TPU v7x, 32 devices: a whole 2x2x4 slice. The times are simulated.
32 devices in a mesh: seq: 8 (over z, y), head: 4 (over x, core).
Axes of the slice: x: 2, y: 2, z: 4, core: 2. Of those that a mesh axis runs over, the one named last changes fastest.
Arguments:
- block_in: bfloat16 [4, 2048, 768], P(None, 'seq'), may hold values from -6 to 6
- cotangent: bfloat16 [4, 2048, 768], P(None, 'seq'), may hold values from -6 to 6
- lengths: int32 [4], replicated, may hold values from 512 to 2048, as said below
- norm_gain: float32 [768], replicated, may hold values from 0.5 to 1.5
- in_proj: float32 [768, 4, 838], P(None, 'head'), may hold values from -0.21875 to 0.21875
- conv_params: float32 [5, 4, 448], P(None, 'head'), may hold values from -2 to 2
- head_params: float32 [3, 24], P(None, 'head'), as said below
- gate_gain: float32 [1536], P('head'), may hold values from 0.5 to 1.5
- out_proj: float32 [1536, 768], P('head'), may hold values from -0.15625 to 0.15625
- norm_gain_momentum: float32 [768], replicated, may hold values from -224 to 224
- in_proj_momentum: float32 [768, 4, 838], P(None, 'head'), may hold values from -112 to 112
- conv_momentum: float32 [5, 4, 448], P(None, 'head'), may hold values from -112 to 112
- head_momentum: float32 [3, 24], P(None, 'head'), may hold values from -512 to 512
- gate_gain_momentum: float32 [1536], P('head'), may hold values from -256 to 256
- out_proj_momentum: float32 [1536, 768], P('head'), may hold values from -384 to 384
- norm_gain_average: float32 [768], replicated, may hold values from 0.5 to 1.5
- in_proj_average: float32 [768, 4, 838], P(None, 'head'), may hold values from -0.21875 to 0.21875
- conv_average: float32 [5, 4, 448], P(None, 'head'), may hold values from -2 to 2
- head_average: float32 [3, 24], P(None, 'head'), may hold values from -1 to 1
- gate_gain_average: float32 [1536], P('head'), may hold values from 0.5 to 1.5
- out_proj_average: float32 [1536, 768], P('head'), may hold values from -0.15625 to 0.15625
Outputs:
- block_out: bfloat16 [4, 2048, 768], P(None, 'seq')
- input_grad: float32 [4, 2048, 768], P(None, 'seq')
- norm_gain_new: float32 [768], replicated
- norm_gain_moment: float32 [768], replicated
- norm_gain_mean: float32 [768], replicated
- in_proj_new: float32 [768, 4, 838], P(None, 'head')
- in_proj_moment: float32 [768, 4, 838], P(None, 'head')
- in_proj_mean: float32 [768, 4, 838], P(None, 'head')
- conv_new: float32 [5, 4, 448], P(None, 'head')
- conv_moment: float32 [5, 4, 448], P(None, 'head')
- conv_mean: float32 [5, 4, 448], P(None, 'head')
- head_new: float32 [3, 24], P(None, 'head')
- head_moment: float32 [3, 24], P(None, 'head')
- head_mean: float32 [3, 24], P(None, 'head')
- gate_gain_new: float32 [1536], P('head')
- gate_gain_moment: float32 [1536], P('head')
- gate_gain_mean: float32 [1536], P('head')
- out_proj_new: float32 [1536, 768], P('head')
- out_proj_moment: float32 [1536, 768], P('head')
- out_proj_mean: float32 [1536, 768], P('head')
Inputs may be any that keep to these rules, and one draw needn't show every extreme that they name: `lengths`: in every draw one sequence has all 2048 slots real. `head_params`: row 0 lies in -5.1 to -4.1, row 1 (log decay rate) in log(0.3 / (2048 * 0.0165)) to log(2), and row 2 in 0.4 to 2.4.
All inputs are finite; a program needn't handle non-finite values.
Results may differ from a plain program's by a relative error of at most 0.01.
The roundings to bfloat16 on the way count: a program that leaves them out, or rounds other values in their place, can miss the bound.
Values may be sent and summed in bfloat16 or wider, within the bound.
No kernel may reach another device: no remote copies, remote signals or barrier semaphores. Data moves between devices by JAX's collectives and lax.ppermute only.
A program may use at most 192 MiB of HBM per device.

v0:
```python
import functools
import math

import jax
import jax.numpy as jnp
from jax import lax
from jax.experimental import pallas as pl
from jax.experimental.pallas import tpu as pltpu
from jax.sharding import PartitionSpec as P

HDIM = 64
CONV = 4
INNER = 1536
EPSILON = 1e-05
MOMENTUM = 0.5
AVERAGE = 0.5
RATES = (0.15, 0.1, 0.5, 0.05, 0.15, 0.02)
HIGHEST = lax.Precision.HIGHEST
F32 = jnp.float32
BF16 = jnp.bfloat16
VMEM = 14
GRP = 4
BLK = 256
HALF = BLK // 2
QUART = BLK // 4
D = 768
ZW = 384
NH = 6
ST = 128
SW = 32
LANES = 128
WCOLS = D // LANES
WROWS = 2 * ZW + 2 * SW
TOK = GRP * BLK
COLS = WROWS + NH
SEG1 = 2 * ZW // GRP
SEG2 = 120
BC_AT, DT_AT, TAP_AT, HD_AT, GG_AT, NG_AT = 384, 448, 456, 464, 472, 473


def nt(a, b, precision=None):
    return lax.dot_general(
        a, b, (((1,), (1,)), ((), ())), preferred_element_type=F32, precision=precision
    )


def nn(a, b, precision=None):
    return lax.dot_general(
        a, b, (((1,), (0,)), ((), ())), preferred_element_type=F32, precision=precision
    )


def tn(a, b, precision=None):
    return lax.dot_general(
        a, b, (((0,), (0,)), ((), ())), preferred_element_type=F32, precision=precision
    )


def iota(shape, dim):
    return lax.broadcasted_iota(jnp.int32, shape, dim)


def split3(value):
    high = value.astype(BF16).astype(F32)
    rest = value - high
    mid = rest.astype(BF16).astype(F32)
    return high, mid, rest - mid


def side_by_side(value, used):
    high, mid, low = split3(jnp.where(iota(value.shape, 1) < used, value, 0.0))
    return (high + pltpu.roll(mid, used, 1) + pltpu.roll(low, 2 * used, 1)).astype(BF16)


def widen(packed, kinds):
    lane, col = iota((LANES, ZW), 0), iota((LANES, ZW), 1)
    goals = [((lane % 32 == col // HDIM + 8 * k) & (lane < 96)).astype(BF16) for k in kinds]
    parts = side_by_side(packed, 32)
    return [nn(parts, goal) for goal in goals]


def head_sums(values):
    goal = (iota((ZW, LANES), 1) == iota((ZW, LANES), 0) // HDIM).astype(BF16)
    high = values.astype(BF16)
    return nn(high, goal) + nn((values - high.astype(F32)).astype(BF16), goal)


def running_sums(triangle, values):
    total = nn(triangle, side_by_side(values, 8))
    total = total + pltpu.roll(total, LANES - 8, 1) + pltpu.roll(total, LANES - 16, 1)
    return jnp.where(iota(total.shape, 1) < 8, total, 0.0)


def lane_mask(which):
    return (iota((1, LANES), 1) // HDIM == which).astype(BF16)


def triangle(lower):
    row, col = iota((BLK, BLK), 0), iota((BLK, BLK), 1)
    return (row >= col if lower else row <= col).astype(BF16)


def call(
    kernel, name, grid, ins, in_specs, outs, out_specs, scratch=(), prefetch=None, flops=0,
    aliases=None, after=(), vmem=VMEM, light=False, token=False,
):
    count = len(ins) + (prefetch is not None)
    results = len(outs)
    if grid == (GRP,) and name not in STREAMED:
        plain, pre, cuts = kernel, count - len(ins), list(in_specs) + list(out_specs)
        used = pre + len(cuts)

        def kernel(*refs):
            at = refs[:pre]
            for i in range(GRP):
                views = [part_of(r, c, i, at) for r, c in zip(refs[pre:used], cuts)]
                STEP.append(i)
                plain(*at, *views, *refs[used:])
                STEP.pop()

        grid = (1,)
        in_specs, out_specs = [whole(a.shape) for a in ins], [whole(a.shape) for a in outs]

    def body(*refs):
        rest = refs[count + len(after) :]
        if token:
            rest[results][...] = jnp.zeros((8, LANES), F32)
            rest = rest[:results] + rest[results + 1 :]
        kernel(*refs[:count], *rest)

    outs, out_specs = list(outs), list(out_specs)
    if token:
        outs.append(sds((8, LANES)))
        out_specs.append(whole((8, LANES)))
    nbytes = sum(math.prod(a.shape) * a.dtype.itemsize for a in (*ins, *outs))
    if light:
        flops, nbytes = 1024, 1024
    spec = pltpu.PrefetchScalarGridSpec(
        num_scalar_prefetch=0 if prefetch is None else 1,
        grid=grid,
        in_specs=list(in_specs) + [pl.BlockSpec(memory_space=pl.ANY)] * len(after),
        out_specs=out_specs,
        scratch_shapes=scratch,
    )
    return pl.pallas_call(
        body,
        grid_spec=spec,
        out_shape=outs,
        compiler_params=pltpu.CompilerParams(
            dimension_semantics=("arbitrary",) * len(grid), vmem_limit_bytes=vmem << 20
        ),
        cost_estimate=pl.CostEstimate(flops=flops, bytes_accessed=nbytes, transcendentals=0),
        input_output_aliases=aliases or {},
        name=name,
    )(*(() if prefetch is None else (prefetch,)), *ins, *after)


STEP = []
STREAMED = ("home_out", "home_grad", "split", "gate", "inner", "edge", "last_x", "local", "back", )


def step_now():
    return STEP[-1] if STEP else pl.program_id(0)


def when(condition):
    if isinstance(condition, bool):
        return lambda body: body() if condition else None
    return pl.when(condition)


def part_of(ref, spec, i, at):
    size = spec.block_shape
    if size is None or tuple(size) == tuple(ref.shape):
        return ref
    cut = []
    for n, length, full in zip(spec.index_map(i, *at), size, ref.shape):
        if length == full:
            cut.append(slice(None))
        elif isinstance(n, int):
            cut.append(pl.ds(n * length, length))
        else:
            cut.append(pl.ds(pl.multiple_of(n * length, length), length))
    return ref.at[tuple(cut)]


def sds(shape, dtype=F32):
    return jax.ShapeDtypeStruct(shape, dtype)


def whole(shape):
    return pl.BlockSpec(shape, lambda *_: (0,) * len(shape))


def rows(width, height=BLK):
    return pl.BlockSpec((height, width), lambda i, *_: (i, 0))


def rows_back(width, height=BLK):
    return pl.BlockSpec((height, width), lambda i, *_: (GRP - 1 - i, 0))


def slot(height, width=D):
    return pl.BlockSpec((1, height, width), lambda i, at: (i ^ at[0], 0, 0))


def pick_kernel(at, *refs):
    for n, goal in enumerate(refs[2 * GRP :]):
        goal[0:HALF, :] = refs[n][0]
        if goal.shape[0] > HALF:
            goal[HALF:, :] = refs[GRP + n][0]


def pick(at, array, edge, after=()):
    def half_of(b):
        return pl.BlockSpec((1, HALF, D), lambda i, at: (at[0] ^ b, at[1], 0))

    def edge_of(b):
        return pl.BlockSpec((1, 16, D), lambda i, at: (at[0] ^ b, BLK // 16 - 1, 0))

    size = HALF + 16 * edge
    specs = [half_of(b) for b in range(GRP)] + [edge_of(b) for b in range(GRP)]
    return call(
        pick_kernel, "pick", (1,), (array,) * (2 * GRP), specs,
        [sds((size, D), BF16)] * GRP, [whole((size, D))] * GRP, prefetch=at, after=after,
    )


def stack_kernel(at, r0, r1, r2, r3, out_ref, *edge):
    refs = (r0, r1, r2, r3)
    for b, ref in enumerate(refs):
        out_ref[b] = ref[0:HALF, :]
    for goal in edge:
        for b, ref in enumerate(refs):

            @when(at[0] ^ b == GRP - 1)
            def _():
                goal[...] = ref[HALF:, :]


def stack(at, parts, after=()):
    size = parts[0].shape[0]
    outs, specs = [sds((GRP, HALF, D), BF16)], [whole((GRP, HALF, D))]
    if size > HALF:
        outs, specs = outs + [sds((16, D), BF16)], specs + [whole((16, D))]
    return call(
        stack_kernel, "stack", (1,), parts, [whole((size, D))] * GRP, outs, specs, prefetch=at, after=after
    )


def prep_kernel(
    win, wout, taps, heads, ng, gg,
    w_ref, wdt_ref, low_ref, send_ref, hp_ref, vec_ref, wide_w, scr, sem,
):
    copy = pltpu.make_async_copy(win.at[:, 0, :], wide_w, sem)
    copy.start()
    low_ref[...] = wout[...].astype(BF16)
    scr[...] = jnp.zeros_like(scr)
    scr[0:3, 0:NH] = heads[...]
    lanes = scr[...]
    for by in (8, 16, 32, 64):
        lanes = lanes + pltpu.roll(lanes, by, 1)
    hp_ref[...] = lanes
    vec_ref[...] = jnp.zeros_like(vec_ref)
    vec_ref[0:1, :] = ng[...].reshape(1, D)
    vec_ref[1:2, 0:ZW] = gg[...].reshape(1, ZW)
    vec_ref[2:3, 0:ZW] = widen(lanes, (0,))[0][2:3, :]
    copy.wait()
    w_ref[...] = wide_w[0:WROWS, :].astype(BF16)
    last = jnp.concatenate([wide_w[WROWS:, :], jnp.zeros((8 - NH, D), F32)], axis=0)
    wdt_ref[...] = jnp.concatenate([last] * 16, axis=0).astype(BF16)
    send_ref[0 : 2 * SW, :] = w_ref[2 * ZW : WROWS, :]
    own = taps[:, 0, :][:, ZW:]
    high = own.astype(BF16).astype(F32)
    mid = (own - high).astype(BF16).astype(F32)
    low = own - high - mid
    parts = jnp.concatenate([high, mid, low, jnp.zeros((1, 2 * SW), F32)], axis=0)
    send_ref[2 * SW :, :] = jnp.zeros((16, D), BF16)
    send_ref[2 * SW :, 0 : 2 * SW] = parts.astype(BF16)


def chunk_of(own_ref, oth_ref, core):
    own, oth = own_ref[0], oth_ref[0]
    first = core == 0
    return jnp.concatenate([jnp.where(first, own, oth), jnp.where(first, oth, own)], axis=0)


def normalise(x, gain):
    u = x.astype(F32)
    scale = lax.rsqrt(jnp.mean(u * u, axis=-1, keepdims=True) + EPSILON)
    return (u * scale * gain).astype(BF16)


def first_kernel(at, own, oth, vecs, wz, wdt, hp, nrm_ref, z_ref, info_ref, row_ref, tot_ref, cum):
    step = step_now()

    @when(step == 0)
    def _():
        cum[...] = jnp.zeros_like(cum)

    normed = normalise(chunk_of(own, oth, at[1]), vecs[0:1, :])
    nrm_ref[...] = normed
    z_ref[...] = nt(normed, wz[...])
    biased = nt(normed, wdt[...]) + hp[0:1, :]
    steps = jax.nn.softplus(biased)
    decays = -jnp.exp(hp[1:2, :]) * steps
    c = running_sums(triangle(True), decays)
    group = iota((BLK, LANES), 1) // 8
    info = jnp.where(group == 0, c, jnp.where(group == 1, steps, biased))
    moved_c = pltpu.roll(c, 24, 1) + cum[0:1, :]
    info_ref[...] = jnp.where(group == 3, moved_c, info)
    row_ref[...] = jnp.transpose(c)[0:8, :]
    cum[0:1, :] = moved_c[BLK - 1 : BLK, :]
    tot_ref[...] = jnp.broadcast_to(cum[0:1, :], (8, LANES))


def mix_kernel(
    at, nrm, halo, vecs, wx, wo, bc0, bc1, bc2, bc3, taps, info,
    mx_ref, px_ref, xa_ref, xdt_ref, mo_ref, po_ref, b_ref, c_ref, h_ref, s_ref,
    wbc, tbc, ext, exto, state,
):
    step = step_now()
    tap = taps[:, 0, :]

    @when(step == 0)
    def _():
        place = jnp.zeros((16, 2 * ST), F32)
        for b, buf in enumerate((bc0, bc1, bc2, bc3)):
            wbc[SW * b : SW * (b + 1), :] = buf[0:SW, :]
            wbc[ST + SW * b : ST + SW * (b + 1), :] = buf[SW : 2 * SW, :]
            at_row, at_col = iota((2 * SW, 2 * ST), 0), iota((2 * SW, 2 * ST), 1)
            goal = jnp.where(at_row < SW, SW * b + at_row, ST + SW * b + at_row - SW)
            put = (at_col == goal).astype(BF16)
            place = place + nn(buf[2 * SW :, 0 : 2 * SW], put)
        tbc[0:5, :] = place[0:5] + place[5:10] + place[10:15]
        before = normalise(jnp.where(at[5] > 0, halo[...], 0.0).astype(BF16), vecs[0:1, :])
        ext[0:8, 0:ZW] = nt(before, wx[...])[8:16]
        ext[0:8, ZW:] = nt(before, wbc[...])[8:16]
        exto[0:8, :] = nt(before, wo[...])[8:16]
        state[...] = jnp.zeros_like(state)

    normed = nrm[...]
    mixed = nt(normed, wx[...])
    mx_ref[...] = mixed
    ext[8:, 0:ZW] = mixed
    ext[8:, ZW:] = nt(normed, wbc[...])
    own = nt(normed, wo[...])
    mo_ref[...] = own
    exto[8:, :] = own
    pre = tap[4:5, 0:ZW]
    pre_bc = tbc[4:5, :]
    pre_o = tap[4:5, ZW:]
    for k in range(CONV):
        pre = pre + tap[k : k + 1, 0:ZW] * ext[5 + k : 5 + k + BLK, 0:ZW]
        pre_bc = pre_bc + tbc[k : k + 1, :] * ext[5 + k : 5 + k + BLK, ZW:]
        pre_o = pre_o + tap[k : k + 1, ZW:] * exto[5 + k : 5 + k + BLK, :]
    px_ref[...] = pre
    po_ref[...] = pre_o
    x = pre * jax.nn.sigmoid(pre)
    xa_ref[...] = x
    bc = (pre_bc * jax.nn.sigmoid(pre_bc)).astype(BF16)
    b_ref[...] = bc[:, 0:ST]
    c_ref[...] = bc[:, ST:]
    ext[0:8, :] = ext[BLK:, :]
    exto[0:8, :] = exto[BLK:, :]

    packed = info[...]
    c = packed[:, 0:LANES]
    keep = iota((BLK, LANES), 1) < 8
    tail = jnp.where(keep, jnp.exp(jnp.where(keep, c[BLK - 1 : BLK, :] - c, 0.0)), 0.0)
    tail_wide, dt_wide = widen(jnp.where(keep, tail, packed), (0, 1))
    xdt = x * dt_wide
    xdt_ref[...] = xdt.astype(BF16)
    fresh = tn((xdt * tail_wide).astype(BF16), bc[:, 0:ST])
    h_ref[0] = state[...]
    for h in range(NH):
        decay = jnp.exp(packed[BLK - 1 : BLK, h : h + 1])
        at = pl.ds(HDIM * h, HDIM)
        state[at, :] = decay * state[at, :] + fresh[HDIM * h : HDIM * (h + 1), :]
    s_ref[...] = state[...].astype(BF16)


def weights_of(h, packed, row, causal):
    diff = packed[:, h : h + 1] - row[h : h + 1, :]
    return jnp.where(causal, jnp.exp(jnp.where(causal, diff, 0.0)), 0.0)


def local_kernel(
    at, xdt, xa, b, c, info, row, hloc, own, oth, low, vecs, yl_ref, dyn_ref, w_ref
):
    step = step_now()
    packed = info[...]
    rowc = row[...]
    causal = iota((BLK, BLK), 0) >= iota((BLK, BLK), 1)
    scores = nt(c[...], b[...])
    c_exp = jnp.exp(jnp.where(iota((BLK, LANES), 1) < 8, packed, 0.0))
    carried = nt(c[...], hloc[0].astype(BF16)) * widen(c_exp, (0,))[0]
    carried = carried + vecs[2:3, 0:ZW] * xa[...]
    for p in range(NH // 2):
        x = xdt[:, LANES * p : LANES * (p + 1)]
        total = carried[:, LANES * p : LANES * (p + 1)]
        for q in range(2):
            weights = (weights_of(2 * p + q, packed, rowc, causal) * scores).astype(BF16)
            total = total + nn(weights, x * lane_mask(q))
        yl_ref[:, LANES * p : LANES * (p + 1)] = total
    place = (at[2] * GRP + step) * BLK + iota((BLK, 1), 0)
    live = place < at[7 + at[0]]
    w = jnp.where(live, chunk_of(own, oth, at[1]), 0.0).astype(BF16)
    w_ref[...] = w
    dyn_ref[...] = nt(w, low[...])


def gate_kernel(at, yl, c, info, hin, z, dyn, vecs, y_ref, sum_ref):
    packed = info[...]
    lane = iota((BLK, LANES), 1)
    cum = jnp.where(lane // 8 == 3, jnp.exp(jnp.where(lane // 8 == 3, packed, 0.0)), 0.0)
    entering = jnp.where(at[5] > 0, hin[...], 0.0).astype(BF16)
    y = yl[...] + nt(c[...], entering) * widen(cum, (3,))[0]
    y_ref[...] = y
    gate = z[...]
    g = y * (gate * jax.nn.sigmoid(gate))
    squares = jnp.sum(g * g, axis=-1, keepdims=True)
    inner = jnp.sum(dyn[...] * vecs[1:2, 0:ZW] * g, axis=-1, keepdims=True)
    both = jnp.where(lane == 0, squares, jnp.where(lane == 1, inner, 0.0))
    sum_ref[...] = jnp.transpose(both)[0:8, :]


def ungate_kernel(
    at, y, z, dyn, s0, s1, s2, s3, info, c, vecs, low,
    dy_ref, dz_ref, yn_ref, p_ref, gg_ref, keep_ref, send_ref, acc,
):
    step = step_now()

    @when(step == 0)
    def _():
        acc[...] = jnp.zeros_like(acc)
        gg_ref[...] = jnp.zeros_like(gg_ref)

    sums = s0[...] + s1[...] + s2[...] + s3[...]
    sums = jnp.transpose(jnp.concatenate([sums, jnp.zeros((LANES - 8, BLK), F32)], axis=0))
    q = lax.rsqrt(sums[:, 0:1] / INNER + EPSILON)
    mean = sums[:, 1:2] * q / INNER
    gate = z[...]
    sigma = jax.nn.sigmoid(gate)
    silu = gate * sigma
    out = y[...]
    g = out * silu
    n = g * q
    d = dyn[...]
    gg = vecs[1:2, 0:ZW]
    d_g = q * (d * gg - n * mean)
    d_y = d_g * silu
    dy_ref[...] = d_y
    dz_ref[...] = (d_g * out * sigma * (1.0 + gate * (1.0 - sigma))).astype(BF16)
    yn = (n * gg).astype(BF16)
    yn_ref[...] = yn
    halves(nn(yn, low[...]).astype(BF16), at[1], keep_ref, send_ref)
    gg_ref[0:1, :] += jnp.sum(d * n, axis=0, keepdims=True)
    packed = info[...]
    lane = iota((BLK, LANES), 1)
    cum = jnp.where(lane // 8 == 3, jnp.exp(jnp.where(lane // 8 == 3, packed, 0.0)), 0.0)
    acc[...] += tn((d_y * widen(cum, (3,))[0]).astype(BF16), c[...])
    p_ref[...] = acc[...].astype(BF16)


def halves(value, core, keep_ref, send_ref):
    low, high = value[0:HALF], value[HALF:]
    first = core == 0
    keep_ref[0] = jnp.where(first, low, high)
    send_ref[0] = jnp.where(first, high, low)


def out_kernel(
    at, yn, w, nrm, dz, g0, g1, g2, g3, acc
):
    step = step_now()

    @when(step == 0)
    def _():
        acc[...] = jnp.zeros_like(acc)

    acc[0:ZW, :] += tn(dz[...], nrm[...])
    acc[ZW:, :] += tn(yn[...], w[...])

    @when(step == GRP - 1)
    def _():
        for b, ref in enumerate((g0, g1, g2, g3)):
            start = pl.multiple_of((at[0] ^ b) * SEG1, SEG1)
            ref[...] = acc[pl.ds(start, SEG1), :].astype(BF16)


def inner_kernel(
    at, xdt, b, c, info, row, dy, hloc, hin, dxi_ref, dbi_ref, dci_ref, dcum_ref, hall_ref
):
    packed = info[...]
    rowc = row[...]
    lane = iota((BLK, LANES), 1)
    causal = iota((BLK, BLK), 0) >= iota((BLK, BLK), 1)
    bb, cc = b[...], c[...]
    scores = nt(cc, bb)
    d_scores = jnp.zeros((BLK, BLK), F32)
    d_cum = jnp.zeros((BLK, LANES), F32)
    columns = []
    dyv = dy[...]
    for p in range(NH // 2):
        x = xdt[:, LANES * p : LANES * (p + 1)]
        d = dyv[:, LANES * p : LANES * (p + 1)].astype(BF16)
        total = jnp.zeros((BLK, LANES), F32)
        for q in range(2):
            h = 2 * p + q
            spans = weights_of(h, packed, rowc, causal)
            d_h = d * lane_mask(q)
            d_spans = nt(d_h, x) * spans
            d_scores = d_scores + d_spans
            both = d_spans * scores
            d_cum = d_cum + jnp.where(lane == h, jnp.sum(both, axis=1, keepdims=True), 0.0)
            columns.append(jnp.sum(both, axis=0, keepdims=True))
            total = total + tn((spans * scores).astype(BF16), d_h)
        dxi_ref[:, LANES * p : LANES * (p + 1)] = total
    columns = jnp.concatenate(columns + [jnp.zeros((LANES - NH, BLK), F32)], axis=0)
    d_cum = d_cum - jnp.transpose(columns)
    low_scores = d_scores.astype(BF16)
    c_exp = jnp.exp(jnp.where(lane < 8, packed, 0.0))
    c_wide = widen(c_exp, (0,))[0]
    base = packed[0:1, 24:32] - packed[0:1, 0:8]
    for h in range(NH):
        here = pl.ds(HDIM * h, HDIM)
        grown = jnp.exp(base[:, h : h + 1]) * hin[here, :].astype(F32)
        grown = jnp.where(at[5] > 0, grown, 0.0)
        hall_ref[0, here, :] = hloc[0, here, :] + grown
    entering = hall_ref[0].astype(BF16)
    carried = nt(cc, entering) * c_wide
    d_cum = d_cum + head_sums(dyv * carried)
    dcum_ref[...] = d_cum
    dci_ref[...] = nn(low_scores, bb) + nn((dyv * c_wide).astype(BF16), entering)
    dbi_ref[...] = tn(low_scores, cc)


def back_kernel(
    at, after, dxi, dbi, dci, dcum, hall, xa, px, b, c, info, dy, hp, vecs,
    dpx_ref, halo_ref, o0, o1, o2, o3, draw_ref, hg_ref, state,
):
    step = step_now()

    @when(step == 0)
    def _():
        state[...] = jnp.where(at[6] > 0, after[...].astype(F32), 0.0)
        hg_ref[...] = jnp.zeros_like(hg_ref)

    packed = info[...]
    lane = iota((BLK, LANES), 1)
    first = lane < 8
    c_last = packed[BLK - 1 : BLK, :]
    tail = jnp.where(first, jnp.exp(jnp.where(first, c_last - packed, 0.0)), 0.0)
    c_exp = jnp.where(first, jnp.exp(jnp.where(first, packed, 0.0)), 0.0)
    mixed = jnp.where(first, tail, jnp.where(lane < 16, packed, pltpu.roll(c_exp, 16, 1)))
    tail_wide, dt_wide, c_wide = widen(mixed, (0, 1, 2))
    x = xa[...]
    xdt = x * dt_wide
    d_y = dy[...]
    bb, cc = b[...], c[...]
    low_state = state[...].astype(BF16)
    d_tail = nt(bb, low_state) * tail_wide
    tails = head_sums(xdt * d_tail)
    d_xdt = dxi[...] + d_tail
    d_b = dbi[...] + nn((xdt * tail_wide).astype(BF16), low_state)
    d_c = dci[...]
    ending = jnp.sum(tails, axis=0, keepdims=True)
    lane1 = iota((1, LANES), 1)
    for h in range(NH):
        here = pl.ds(HDIM * h, HDIM)
        inner = jnp.sum(state[here, :] * hall[0, here, :], axis=(0, 1), keepdims=True)
        ending = ending + jnp.where(lane1 == h, inner * jnp.exp(c_last[:, h : h + 1]), 0.0)
    d_cum = dcum[...] - tails
    d_cum = d_cum + jnp.where(iota((BLK, LANES), 0) == BLK - 1, ending, 0.0)
    d_a = running_sums(triangle(False), d_cum)
    fresh = tn((d_y * c_wide).astype(BF16), cc)
    for h in range(NH):
        here = pl.ds(HDIM * h, HDIM)
        decay = jnp.exp(c_last[:, h : h + 1])
        state[here, :] = decay * state[here, :] + fresh[HDIM * h : HDIM * (h + 1), :]
    rate = -jnp.exp(hp[1:2, :])
    d_dt = head_sums(x * d_xdt) + rate * d_a
    biased = pltpu.roll(packed, LANES - 16, 1)
    steps = pltpu.roll(packed, LANES - 8, 1)
    used = lane < NH
    d_raw = jnp.where(used, d_dt * jax.nn.sigmoid(jnp.where(used, biased, 0.0)), 0.0)
    draw_ref[...] = d_raw.astype(BF16)
    hg_ref[0:1, :] += jnp.sum(d_raw, axis=0, keepdims=True)
    g_rate = jnp.where(used, d_a * rate * jnp.where(used, steps, 0.0), 0.0)
    hg_ref[1:2, :] += jnp.sum(g_rate, axis=0, keepdims=True)
    hg_ref[2:3, :] += jnp.sum(head_sums(d_y * x), axis=0, keepdims=True)
    d_x = d_xdt * dt_wide + vecs[2:3, 0:ZW] * d_y
    pre = px[...]
    sigma = jax.nn.sigmoid(pre)
    d_pre = d_x * sigma * (1.0 + pre * (1.0 - sigma))
    dpx_ref[...] = d_pre
    halo_ref[...] = d_pre[0:8]
    for s, ref in enumerate((o0, o1, o2, o3)):
        for n, value in enumerate((d_b, d_c)):
            mine = value[:, SW * s : SW * (s + 1)].astype(BF16)
            ref[:, SW * n : SW * (n + 1)] = mine[0:HALF]
            ref[:, SW * (n + 2) : SW * (n + 3)] = mine[HALF:]


def edge_kernel(o0, r1, r2, r3, po, halo_x, dpo_ref, halo_ref):
    d = o0[...].astype(F32) + r1[...].astype(F32) + r2[...].astype(F32) + r3[...].astype(F32)
    d = jnp.concatenate([d[:, 0 : 2 * SW], d[:, 2 * SW :]], axis=0)
    pre = po[...]
    sigma = jax.nn.sigmoid(pre)
    d = d * sigma * (1.0 + pre * (1.0 - sigma))
    dpo_ref[...] = d

    @when(step_now() == 0)
    def _():
        halo_ref[:, X_LANES] = halo_x[...]
        halo_ref[:, ZW:] = jnp.zeros((8, LANES), F32)
        halo_ref[:, O_LANES] = d[0:8]


def unconvolve(acc, ext, d_pre, follows, values, tap, lanes):
    ext[0:BLK, :] = d_pre
    ext[BLK:, :] = follows
    total = jnp.zeros(d_pre.shape, F32)
    for k in range(CONV):
        shifted = ext[3 - k : 3 - k + BLK, :]
        total = total + tap[k : k + 1, lanes] * shifted
        acc[TAP_AT + k : TAP_AT + k + 1, lanes] += jnp.sum(values * shifted, axis=0, keepdims=True)
    acc[TAP_AT + CONV : TAP_AT + CONV + 1, lanes] += jnp.sum(d_pre, axis=0, keepdims=True)
    return total


X_LANES, O_LANES = slice(0, ZW), slice(ZW, ZW + 2 * SW)


END = 16


def last_x_kernel(
    at, dpx, nx, mx, taps, dz, draw, nrm, w, wdt, pb_ref, end_ref, acc, ext
):
    step = step_now()

    @when(step == 0)
    def _():
        acc[...] = jnp.zeros_like(acc)

    follows = jnp.where(step < GRP - 1, nx[...], 0.0)
    d_mx = unconvolve(acc, ext, dpx[...], follows, mx[...], taps[:, 0, :], X_LANES)
    end_ref[...] = d_mx[BLK - END :, :]
    late = (step == GRP - 1) & (iota((BLK, 1), 0) >= BLK - END)
    p_x = jnp.where(late, 0.0, d_mx).astype(BF16)
    p_t = draw[...]
    pb_ref[...] = nn(dz[...], w[0:ZW, :]) + nn(p_x, w[ZW:, :]) + nn(p_t, wdt[...])
    normed = nrm[...]
    acc[0:ZW, :] += tn(p_x, normed)
    acc[DT_AT : DT_AT + 8, :] += tn(p_t, normed)[0:8]


def last_o_kernel(
    at, dpo, no, halo, mo, taps, nrm, w, wx, pb, vecs, gg, hg, acc_in, end, mxe,
    keep_ref, send_ref, g0, g1, g2, g3, ext, acc, wide_pb,
):
    step = step_now()

    @when(step == 0)
    def _():
        acc[...] = acc_in[...]
        acc[HD_AT : HD_AT + 8, 0:LANES] = hg[...]
        acc[GG_AT : GG_AT + 1, 0:ZW] = gg[0:1, :]

    after = jnp.where(at[6] > 0, halo[...], 0.0)
    follows = jnp.where(step < GRP - 1, no[...], after[:, O_LANES])
    p_o = unconvolve(acc, ext, dpo[...], follows, mo[...], taps[:, 0, :], O_LANES).astype(BF16)
    wide_pb[...] = pb[...] + nn(p_o, w[...])
    normed = nrm[...]

    @when(step == GRP - 1)
    def _():
        rows_after = jnp.concatenate([jnp.zeros((END, ZW), F32), after[:, X_LANES]], axis=0)
        total = end[...]
        for k in range(CONV):
            shifted = rows_after[3 - k : 3 - k + END, :]
            total = total + taps[k : k + 1, 0, X_LANES] * shifted
            grad = jnp.sum(mxe[...] * shifted, axis=0, keepdims=True)
            acc[TAP_AT + k : TAP_AT + k + 1, X_LANES] += grad
        p_x = total.astype(BF16)
        wide_pb[BLK - END :, :] += nn(p_x, wx[...])
        acc[0:ZW, :] += tn(p_x, normed[BLK - END :, :])

    back = wide_pb[...]
    halves(back.astype(BF16), at[1], keep_ref, send_ref)
    acc[NG_AT : NG_AT + 1, :] += jnp.sum(back * normed.astype(F32), axis=0, keepdims=True)
    acc[BC_AT:DT_AT, :] += tn(p_o, normed)

    @when(step == GRP - 1)
    def _():
        acc[NG_AT : NG_AT + 1, :] = acc[NG_AT : NG_AT + 1, :] / vecs[0:1, :]
        for b, ref in enumerate((g0, g1, g2, g3)):
            start = pl.multiple_of((at[0] ^ b) * SEG2, 8)
            ref[...] = acc[pl.ds(start, SEG2), :].astype(BF16)


def split_kernel(at, keep, other, keep_ref, send_ref):
    value = keep[0].astype(F32) + other[0].astype(F32)
    low, high = value[0:QUART], value[QUART:]
    first = at[4] == 0
    keep_ref[0] = jnp.where(first, low, high)
    send_ref[0] = jnp.where(first, high, low).astype(BF16)


def add_kernel(keep, other, r0, r1, r2, r3):
    for b, ref in enumerate((r0, r1, r2, r3)):
        ref[...] = (keep[b] + other[b].astype(F32)).astype(BF16)


def sum_kernel(*refs):
    total = refs[0][...].astype(F32)
    for ref in refs[1:-1]:
        total = total + ref[...].astype(F32)
    refs[-1][...] = total.astype(refs[-1].dtype)


def place_quarters(at, b, parts, scr):
    core, xbit = at[1], at[4]
    for n, ref in enumerate(parts):
        half = core if n < 2 else 1 - core
        quarter = xbit if n % 2 == 0 else 1 - xbit
        start = pl.multiple_of(half * HALF + quarter * QUART, QUART)
        scr[pl.ds(start, QUART), :] = ref[0]


def home_out_kernel(at, block, a, x, ac, xc, out_ref, scr):
    step = step_now()
    place_quarters(at, step, (a, x, ac, xc), scr)
    place = (at[2] * GRP + at[0]) * BLK + iota((BLK, 1), 0)
    live = place < at[7 + step]
    total = block[0].astype(F32) + scr[...].astype(F32)
    out_ref[0] = jnp.where(live, total, 0.0).astype(BF16)


def home_grad_kernel(at, block, cot, vecs, a, x, ac, xc, out_ref, scr):
    step = step_now()
    place_quarters(at, step, (a, x, ac, xc), scr)
    place = (at[2] * GRP + at[0]) * BLK + iota((BLK, 1), 0)
    live = place < at[7 + step]
    u = block[0].astype(F32)
    scale = lax.rsqrt(jnp.mean(u * u, axis=-1, keepdims=True) + EPSILON)
    m = u * scale
    f = scr[...].astype(F32) * vecs[0:1, :]
    inner = jnp.mean(f * m, axis=-1, keepdims=True)
    out_ref[0] = scale * (f - m * inner) + jnp.where(live, cot[0].astype(F32), 0.0)


def home(kernel, name, at, arrays, specs, parts, dtype, after=()):
    full = pl.BlockSpec((1, BLK, D), lambda i, *_: (i, 0, 0))
    part = pl.BlockSpec((1, QUART, D), lambda i, at: (i ^ at[0], 0, 0))
    specs = [full if s is None else whole(s) for s in specs]
    return call(
        kernel, name, (GRP,), (*arrays, *parts), specs + [part] * 4, [sds((GRP, BLK, D), dtype)],
        [full], scratch=[pltpu.VMEM((BLK, D), BF16)], prefetch=at, after=after, token=True,
    )


def advance(weight, gradient, moment, average, rate):
    moment_new = MOMENTUM * moment + gradient
    weight_new = weight - rate * (gradient + MOMENTUM * moment_new)
    average_new = AVERAGE * average + (1.0 - AVERAGE) * weight_new
    return (weight_new, moment_new, average_new)


def stepped(grad_of, weights, outs, blocks, buffers, sems, rate):
    ins, done = buffers[:3], buffers[3:]

    def reads(n):
        start, size = blocks[n]
        return [
            pltpu.make_async_copy(
                w.at[pl.ds(start, size), 0, :], buf.at[pl.ds(start, size), :], sems.at[n, j]
            )
            for j, (w, buf) in enumerate(zip(weights, ins))
        ]

    def writes(n):
        start, size = blocks[n]
        return [
            pltpu.make_async_copy(
                buf.at[pl.ds(start, size), :], o.at[pl.ds(start, size), 0, :], sems.at[n, 3 + j]
            )
            for j, (o, buf) in enumerate(zip(outs, done))
        ]

    for n in range(len(blocks)):
        for copy in reads(n):
            copy.start()
    for n, (start, size) in enumerate(blocks):
        for copy in reads(n):
            copy.wait()
        here = pl.ds(start, size)
        new = advance(ins[0][here, :], grad_of(n), ins[1][here, :], ins[2][here, :], rate)
        for buf, value in zip(done, new):
            buf[here, :] = value
        for copy in writes(n):
            copy.start()
    for n in range(len(blocks)):
        for copy in writes(n):
            copy.wait()


Z_BLOCKS = tuple((96 * n, 96) for n in range(4))
X_BLOCKS = tuple((ZW + 96 * n, 96) for n in range(4)) + ((2 * ZW, COLS - 2 * ZW),)


def update_a_kernel(
    at, g0, g1, g2, g3, w, m, a, wi, mi, ai, x0, x1, x2, w_ref, m_ref, a_ref, wo, mo, ao,
    grad, b0, b1, b2, b3, b4, b5, sems, *, rate, rate_in,
):
    for b, ref in enumerate((g0, g1, g2, g3)):
        grad[pl.ds(pl.multiple_of((at[0] ^ b) * SEG1, SEG1), SEG1), :] = ref[0:SEG1, :].astype(F32)
    stepped(
        lambda n: grad[96 * n : 96 * (n + 1), :], (wi, mi, ai), (wo, mo, ao), Z_BLOCKS,
        (b0, b1, b2, b3, b4, b5), sems, rate_in,
    )
    w_ref[...], m_ref[...], a_ref[...] = advance(w[...], grad[ZW:, :], m[...], a[...], rate)


def update_b_kernel(
    at, g0, g1, g2, g3, wi, mi, ai, wo, mo, ao,
    grad, b0, b1, b2, b3, b4, b5, sems, *, rate,
):
    for b, ref in enumerate((g0, g1, g2, g3)):
        start = pl.multiple_of((at[0] ^ b) * SEG2, 8)
        grad[pl.ds(start, SEG2), :] = ref[...].astype(F32)
    stepped(
        lambda n: grad[96 * n : min(96 * (n + 1), COLS - ZW), :], (wi, mi, ai), (wo, mo, ao), X_BLOCKS,
        (b0, b1, b2, b3, b4, b5), sems, rate,
    )


SMALL = GRP * SEG2 - TAP_AT


def small_kernel(at, g0, g1, g2, g3, small_ref, norm_ref):
    for b, ref in enumerate((g0, g1, g2, g3)):

        @when(at[0] ^ b == GRP - 1)
        def _():
            small_ref[...] = ref[SEG2 - SMALL :, :].astype(F32)
            norm_ref[...] = ref[SEG2 - 8 :, :].astype(F32)


def add_small_kernel(a, b, out_ref):
    out_ref[...] = a[...] + b[...]


def update_small_kernel(
    small, n0, n1, ng, ngm, nga, cv, cvm, cva, hd, hdm, hda, gg, ggm, gga, *outs, rates
):
    ng_o, cv_o, hd_o, gg_o = (outs[3 * n : 3 * n + 3] for n in range(4))
    at_norm = NG_AT - TAP_AT - (SMALL - 8)
    norms = [n[at_norm : at_norm + 1, :] for n in (n0, n1)]
    grad = (norms[0] + norms[1]).reshape(D)
    for ref, new in zip(ng_o, advance(ng[...], grad, ngm[...], nga[...], rates[0])):
        ref[...] = new
    grad = small[0:5, 0 : ZW + 2 * SW]
    old = [a[:, 0, :] for a in (cv, cvm, cva)]
    for ref, new in zip(cv_o, advance(old[0], grad, old[1], old[2], rates[2])):
        ref[:, 0, :] = new
    at_head = HD_AT - TAP_AT
    grad = small[at_head : at_head + 3, 0:NH]
    for ref, new in zip(hd_o, advance(hd[...], grad, hdm[...], hda[...], rates[3])):
        ref[...] = new
    at_gate = GG_AT - TAP_AT
    grad = small[at_gate : at_gate + 1, 0:ZW].reshape(ZW)
    for ref, new in zip(gg_o, advance(gg[...], grad, ggm[...], gga[...], rates[4])):
        ref[...] = new


def trade(axis, flip):
    count = lax.axis_size(axis)
    pairs = [(i, i ^ flip) for i in range(count)]
    return lambda array: lax.ppermute(array, axis, pairs)


def moved(array, by):
    count = lax.axis_size("seq")
    if count == 2 * abs(by):
        return trade("seq", abs(by))(array)
    pairs = [(i, i + by) for i in range(count) if 0 <= i + by < count]
    return lax.ppermute(array, "seq", pairs)


def grow(decay, state):
    return jnp.repeat(decay[0, 24 : 24 + NH], HDIM)[:, None] * state


def pieces_before(state, logs, way):
    count = lax.axis_size("seq") // GRP
    found = moved(state, way * GRP)
    by = 1
    if count > 2:
        there = lax.axis_index("seq") // GRP
        decay = moved(jnp.exp(logs), way * GRP)
        total = found.astype(F32)
        while by < count - 1:
            inside = (there >= by) if way > 0 else (there + by < count)
            earlier = moved(total.astype(BF16), way * GRP * by).astype(F32)
            total = jnp.where(inside, grow(decay, earlier) + total, total)
            decay = decay * moved(decay, way * GRP * by)
            by *= 2
        found = total.astype(BF16)
    return found


def group_sum(parts, height, after=()):
    return add_rows(height, [parts[0]] + [trade("seq", b)(parts[b]) for b in (1, 2, 3)], after)


def add_rows(height, arrays, after=()):
    spec = whole((height, D))
    out = [sds((height, D), BF16)]
    return call(sum_kernel, "sum", (1,), arrays, [spec] * len(arrays), out, [spec], after=after)[0]


def across_groups(mine, height, after=()):
    by = GRP
    while by < lax.axis_size("seq"):
        mine = add_rows(height, [mine, trade("seq", by)(mine)], after)
        by *= 2
    return mine


def all_quarters(mine):
    return [mine] + [trade("seq", b)(mine) for b in (1, 2, 3)]


def slot_of(height):
    return pl.BlockSpec((1, height, D), lambda i, at: (i, 0, 0))


def split_both(at, keep, other, after=()):
    return call(
        split_kernel, "split", (GRP,), (keep, other), [slot_of(HALF)] * 2,
        [sds((GRP, QUART, D)), sds((GRP, QUART, D), BF16)], [slot_of(QUART)] * 2,
        prefetch=at, after=after,
    )


def quarter_add(keep, other, after=()):
    every = whole((GRP, QUART, D))
    return call(
        add_kernel, "add", (1,), (keep, other), [every] * 2,
        [sds((QUART, D), BF16)] * 4, [whole((QUART, D))] * 4, after=after,
    )


def join_kernel(r0, r1, r2, r3, out_ref):
    for b, ref in enumerate((r0, r1, r2, r3)):
        out_ref[b] = ref[ref.shape[0] - QUART :, :]


def quarter_home(parts, after=()):
    return join([parts[0]] + [trade("seq", b)(parts[b]) for b in (1, 2, 3)], after)


def join(got, after=()):
    return call(
        join_kernel, "join", (1,), got, [whole(a.shape) for a in got],
        [sds((GRP, QUART, D), BF16)], [whole((GRP, QUART, D))], after=after,
    )[0]


def all_home(a):
    x = trade("head", 2)(a)
    return a, x, trade("head", 1)(a), trade("head", 1)(x)


def shards(
    block_in, cotangent, lengths,
    norm_gain, in_proj, conv_params, head_params, gate_gain, out_proj,
    norm_gain_momentum, in_proj_momentum, conv_momentum, head_momentum, gate_gain_momentum,
    out_proj_momentum,
    norm_gain_average, in_proj_average, conv_average, head_average, gate_gain_average,
    out_proj_average,
):
    seq_at, head_at = lax.axis_index("seq"), lax.axis_index("head")
    place = seq_at % GRP
    groups = lax.axis_size("seq") // GRP
    group = seq_at // GRP
    at = [place, head_at % 2, group, 0, head_at // 2, group > 0, group < groups - 1]
    at = jnp.concatenate([jnp.stack([jnp.asarray(v, jnp.int32) for v in at]), lengths])

    def turned(array):
        return jnp.transpose(array, (2, 1, 0))

    once = lengths[0] >= 0

    def apart(step):
        shapes = jax.eval_shape(step)
        return lax.cond(
            once, step, lambda: jax.tree.map(lambda s: jnp.zeros(s.shape, s.dtype), shapes)
        )

    anyspec = pl.BlockSpec(memory_space=pl.ANY)

    picked = pick(at, block_in, True)
    got = [picked[0]] + [trade("seq", b)(picked[b]) for b in (1, 2, 3)]
    w, wdt, low, send_bc, hp, vecs = call(
        prep_kernel, "prep", (1,),
        (turned(in_proj), out_proj, conv_params, head_params, norm_gain, gate_gain),
        [anyspec, whole((ZW, D)), whole((5, 1, 448)), whole((3, NH)), whole((D,)), whole((ZW,))],
        [sds((WROWS, D), BF16), sds((LANES, D), BF16), sds((ZW, D), BF16), sds((80, D), BF16),
         sds((8, LANES)), sds((8, D))],
        [whole((WROWS, D)), whole((LANES, D)), whole((ZW, D)), whole((80, D)), whole((8, LANES)), whole((8, D))],
        scratch=[pltpu.VMEM((COLS, D), F32), pltpu.VMEM((8, LANES), F32), pltpu.SemaphoreType.DMA],
        after=(picked[0],),
    )
    bcs = [send_bc] + [trade("head", b)(send_bc) for b in (1, 2, 3)]
    own, edge = stack(at, got, (w,))
    oth = trade("head", 1)(own)
    halo = moved(edge, GRP)
    cot_picked = pick(at, cotangent, False, (own,))
    cot_got = [cot_picked[0]] + [trade("seq", b)(cot_picked[b]) for b in (1, 2, 3)]

    def wblock(n, height):
        return pl.BlockSpec((height, D), lambda i, *_: (n, 0))

    nrm, z, info, rowc, logs = call(
        first_kernel, "first", (GRP,), (own, oth, vecs, w, wdt, hp),
        [slot(HALF), slot(HALF), whole((8, D)), wblock(0, ZW), whole((LANES, D)), whole((8, LANES))],
        [sds((TOK, D), BF16), sds((TOK, ZW)), sds((TOK, LANES)), sds((8, TOK)), sds((8, LANES))],
        [rows(D), rows(ZW), rows(LANES), pl.BlockSpec((8, BLK), lambda i, *_: (0, i)), whole((8, LANES))],
        scratch=[pltpu.VMEM((8, LANES), F32)], prefetch=at, flops=2 * TOK * D * 512, after=(halo, *bcs[1:]),
    )
    hspec = pl.BlockSpec((1, ZW, ST), lambda i, *_: (i, 0, 0))
    rowspec = pl.BlockSpec((8, BLK), lambda i, *_: (0, i))
    mx, px, xa, xdt, mo, po, bb, cc, hloc, fresh = call(
        mix_kernel, "mix", (GRP,), (nrm, halo, vecs, w, w, *bcs, conv_params, info),
        [rows(D), whole((16, D)), whole((8, D)), wblock(1, ZW), wblock(12, 2 * SW)]
        + [whole((80, D))] * 4 + [whole((5, 1, 448)), rows(LANES)],
        [sds((TOK, ZW)), sds((TOK, ZW)), sds((TOK, ZW)), sds((TOK, ZW), BF16), sds((TOK, 2 * SW)),
         sds((TOK, 2 * SW)), sds((TOK, ST), BF16), sds((TOK, ST), BF16), sds((GRP, ZW, ST)),
         sds((ZW, ST), BF16)],
        [rows(ZW), rows(ZW), rows(ZW), rows(ZW), rows(2 * SW), rows(2 * SW), rows(ST), rows(ST),
         hspec, whole((ZW, ST))],
        scratch=[pltpu.VMEM((2 * ST, D), BF16), pltpu.VMEM((8, 2 * ST), F32),
                 pltpu.VMEM((BLK + 8, ZW + 2 * ST), F32), pltpu.VMEM((BLK + 8, 2 * SW), F32),
                 pltpu.VMEM((ZW, ST), F32)],
        flops=2 * TOK * D * 704, prefetch=at,
    )
    hin = pieces_before(fresh, logs, 1)
    cot_own = stack(at, cot_got, (fresh,))[0]
    cot_oth = trade("head", 1)(cot_own)
    yl, dyn, w_live = call(
        local_kernel, "local", (GRP,),
        (xdt, xa, bb, cc, info, rowc, hloc, cot_own, cot_oth, low, vecs),
        [rows(ZW), rows(ZW), rows(ST), rows(ST), rows(LANES), rowspec, hspec, slot(HALF),
         slot(HALF), whole((ZW, D)), whole((8, D))],
        [sds((TOK, ZW)), sds((TOK, ZW)), sds((TOK, D), BF16)], [rows(ZW), rows(ZW), rows(D)],
        prefetch=at, flops=2 * TOK * (D * ZW + 4 * BLK * ZW),
    )
    y, sums = call(
        gate_kernel, "gate", (GRP,), (yl, cc, info, hin, z, dyn, vecs),
        [rows(ZW), rows(ST), rows(LANES), whole((ZW, ST)), rows(ZW), rows(ZW), whole((8, D))],
        [sds((TOK, ZW)), sds((8, TOK))], [rows(ZW), rowspec], prefetch=at, flops=2 * TOK * ST * ZW,
    )
    all_sums = [sums] + [trade("head", b)(sums) for b in (1, 2, 3)]
    half_slot = pl.BlockSpec((1, HALF, D), lambda i, at: (i ^ at[0], 0, 0))
    dy, dz, yn, pulled, g_gate, keep, send = call(
        ungate_kernel, "ungate", (GRP,), (y, z, dyn, *all_sums, info, cc, vecs, low),
        [rows(ZW)] * 3 + [rowspec] * 4 + [rows(LANES), rows(ST), whole((8, D)), whole((ZW, D))],
        [sds((TOK, ZW)), sds((TOK, ZW), BF16), sds((TOK, ZW), BF16), sds((ZW, ST), BF16), sds((8, ZW))]
        + [sds((GRP, HALF, D), BF16)] * 2,
        [rows(ZW), rows(ZW), rows(ZW), whole((ZW, ST)), whole((8, ZW))] + [half_slot] * 2,
        scratch=[pltpu.VMEM((ZW, ST), F32)], flops=2 * TOK * (ST + D) * ZW, prefetch=at,
    )
    grads1 = call(
        out_kernel, "out", (GRP,), (yn, w_live, nrm, dz), [rows(ZW), rows(D), rows(D), rows(ZW)],
        [sds((SEG1, D), BF16)] * 4, [whole((SEG1, D))] * 4,
        scratch=[pltpu.VMEM((2 * ZW, D), F32)], prefetch=at, flops=4 * TOK * D * ZW,
    )
    got1 = [trade("seq", b)(grads1[b]) for b in (1, 2, 3)]
    keep2, send2 = split_both(at, keep, trade("head", 1)(send), (grads1[0],))
    other2 = trade("head", 2)(send2)
    hback = pl.BlockSpec((1, ZW, ST), lambda i, *_: (GRP - 1 - i, 0, 0))

    after = pieces_before(pulled, logs, -1)
    dxi, dbi, dci, dcum, hall = call(
        inner_kernel, "inner", (GRP,), (xdt, bb, cc, info, rowc, dy, hloc, hin),
        [rows(ZW), rows(ST), rows(ST), rows(LANES), rowspec, rows(ZW), hspec, whole((ZW, ST))],
        [sds((TOK, ZW)), sds((TOK, ST)), sds((TOK, ST)), sds((TOK, LANES)), sds((GRP, ZW, ST))],
        [rows(ZW), rows(ST), rows(ST), rows(LANES), hspec], prefetch=at, after=(send2,),
    )
    dpx, halo_x, *dbc, draw, g_head = call(
        back_kernel, "back", (GRP,),
        (after, dxi, dbi, dci, dcum, hall, xa, px, bb, cc, info, dy, hp, vecs),
        [whole((ZW, ST)), rows_back(ZW), rows_back(ST), rows_back(ST), rows_back(LANES), hback,
         rows_back(ZW), rows_back(ZW), rows_back(ST), rows_back(ST), rows_back(LANES),
         rows_back(ZW), whole((8, LANES)), whole((8, D))],
        [sds((TOK, ZW)), sds((8, ZW))] + [sds((TOK // 2, LANES), BF16)] * 4 + [sds((TOK, LANES), BF16), sds((8, LANES))],
        [rows_back(ZW), whole((8, ZW))] + [rows_back(LANES, HALF)] * 4 + [rows_back(LANES), whole((8, LANES))],
        scratch=[pltpu.VMEM((ZW, ST), F32)], flops=2 * TOK * 4 * ST * ZW, prefetch=at,
    )
    quarters = quarter_add(keep2, other2, (g_head,))
    one, joint = whole((SEG1, D)), whole((SEG1 + QUART, D))
    mine1 = add_rows(SEG1, [grads1[0], *got1], (g_head,))

    def after_rows(width):
        last = TOK // 8 - 1
        return pl.BlockSpec((8, width), lambda i, *_: (min((i + 1) * (BLK // 8), last) if isinstance(i, int) else jnp.minimum((i + 1) * (BLK // 8), last), 0))

    final = GRP * SEG2
    half_rows = pl.BlockSpec((1, HALF, D), lambda i, at: (i ^ at[0], 0, 0))

    bc_got = [trade("head", b)(dbc[b]) for b in (1, 2, 3)]
    pb, end, acc = call(
        last_x_kernel, "last_x", (GRP,),
        (dpx, dpx, mx, conv_params, dz, draw, nrm, w, wdt),
        [rows(ZW), after_rows(ZW), rows(ZW), whole((5, 1, 448)), rows(ZW), rows(LANES),
         rows(D), whole((2 * ZW, D)), whole((LANES, D))],
        [sds((TOK, D)), sds((END, ZW)), sds((final, D))], [rows(D), whole((END, ZW)), whole((final, D))],
        scratch=[pltpu.VMEM((BLK + 8, ZW), F32)], prefetch=at, flops=4 * TOK * D * 2 * ZW, after=(mine1, quarters[0]),
    )
    dpo, halo_o = call(
        edge_kernel, "edge", (GRP,), (dbc[0], *bc_got, po, halo_x),
        [rows(LANES, HALF)] * 4 + [rows(2 * SW), whole((8, ZW))],
        [sds((TOK, 2 * SW)), sds((8, ZW + LANES))], [rows(2 * SW), whole((8, ZW + LANES))], after=(acc,),
    )
    halo_o = moved(halo_o, -GRP)
    total1 = across_groups(mine1, SEG1, (halo_o,))
    keep_b, send_b, *grads2 = call(
        last_o_kernel, "last_o", (GRP,),
        (dpo, dpo, halo_o, mo, conv_params, nrm, w, w, pb, vecs, g_gate, g_head, acc, end, mx),
        [rows(2 * SW), after_rows(2 * SW), whole((8, ZW + LANES)), rows(2 * SW), whole((5, 1, 448)), rows(D),
         wblock(12, 2 * SW), wblock(1, ZW), rows(D), whole((8, D)), whole((8, ZW)), whole((8, LANES)), whole((final, D)),
         whole((END, ZW)), pl.BlockSpec((END, ZW), lambda i, *_: (TOK // END - 1, 0))],
        [sds((GRP, HALF, D), BF16)] * 2 + [sds((SEG2, D), BF16)] * 4,
        [half_rows] * 2 + [whole((SEG2, D))] * 4,
        scratch=[pltpu.VMEM((BLK + 8, 2 * SW), F32), pltpu.VMEM((final, D), F32), pltpu.VMEM((BLK, D), F32)],
        prefetch=at, flops=4 * TOK * D * 2 * SW, after=(total1,),
    )

    def finish():
        keep3, send3 = split_both(at, keep_b, trade("head", 1)(send_b))
        quarters_b = quarter_add(keep3, trade("head", 2)(send3))
        mine2 = group_sum(grads2, SEG2, (quarters_b[0],))
        return quarters_b, mine2, quarter_home(quarters, (mine2,))

    quarters_b, mine2, own_out = apart(finish)
    x_out = trade("head", 2)(own_out)
    root = math.sqrt(TOK * lax.axis_size("seq"))
    mat = whole((ZW, D))
    turned3 = [turned(p) for p in (in_proj, in_proj_momentum, in_proj_average)]
    turned_shape = [sds((COLS, 1, D))] * 3
    buffers = [pltpu.VMEM((COLS, D), F32)] * 6 + [pltpu.SemaphoreType.DMA((5, 6))]
    hbm = pl.BlockSpec(memory_space=pltpu.HBM)

    def gather():
        own_grad = quarter_home(quarters_b)
        return own_grad, across_groups(mine2, SEG2, (own_grad,))

    own_grad, total2 = apart(gather)
    sums1 = all_quarters(total1)
    def spread_out():
        x_grad = trade("head", 2)(own_grad)
        core_grad, sums2 = trade("head", 1)(own_grad), all_quarters(total2)
        parts = (own_out, x_out, trade("head", 1)(own_out), trade("head", 1)(x_out))
        block_out, _ = home(home_out_kernel, "home_out", at, (block_in,), (None,), parts, BF16)
        return x_grad, core_grad, sums2, block_out

    x_grad, core_grad, sums2, block_out = apart(spread_out)
    grad_parts = (own_grad, x_grad, core_grad, trade("head", 1)(x_grad))

    quarter = whole((SEG2, D))
    small, norm = call(
        small_kernel, "small", (1,), sums2, [quarter] * 4, [sds((SMALL, D)), sds((8, D))],
        [whole((SMALL, D)), whole((8, D))], prefetch=at,
    )
    eight = whole((8, D))
    norm = call(
        add_small_kernel, "add_small", (1,), (norm, trade("head", 1)(norm)), [eight] * 2, [sds((8, D))], [eight]
    )[0]
    norms = [norm, trade("head", 2)(norm)]
    *in_half, done_b = call(
        functools.partial(update_b_kernel, rate=RATES[1] / root), "update_b", (1,),
        (*sums2, *turned3), [quarter] * 4 + [hbm] * 3, turned_shape, [hbm] * 3,
        scratch=[pltpu.VMEM((GRP * SEG2, D), F32)] + buffers, prefetch=at,
        after=(norm,), vmem=56, token=True,
    )
    input_grad, done_grad = home(
        home_grad_kernel, "home_grad", at, (block_in, cotangent, vecs), (None, None, (8, D)),
        grad_parts, F32, (done_b,),
    )
    out_w, out_m, out_a, *in_new, done_a = call(
        functools.partial(update_a_kernel, rate=RATES[5] / root, rate_in=RATES[1] / root), "update_a", (1,),
        (*sums1, out_proj, out_proj_momentum, out_proj_average, *turned3, *in_half),
        [one] * 4 + [mat] * 3 + [hbm] * 6, [sds((ZW, D))] * 3 + turned_shape,
        [mat] * 3 + [hbm] * 3, scratch=[pltpu.VMEM((2 * ZW, D), F32)] + buffers, prefetch=at,
        after=(done_grad,), aliases={11: 3, 12: 4, 13: 5}, vmem=56, token=True,
    )
    groups_of = (
        (norm_gain, norm_gain_momentum, norm_gain_average),
        (conv_params, conv_momentum, conv_average),
        (head_params, head_momentum, head_average),
        (gate_gain, gate_gain_momentum, gate_gain_average),
    )
    arrays = [a for three in groups_of for a in three]
    specs = [whole(a.shape) for a in arrays]
    new = call(
        functools.partial(update_small_kernel, rates=[r / root for r in RATES]), "update_small", (1,),
        (small, *norms, *arrays), [whole((SMALL, D))] + [whole((8, D))] * 2 + specs,
        [sds(a.shape) for a in arrays], specs, after=(done_a,),
    )
    ng3, cv3, hd3, gg3 = (tuple(new[3 * n : 3 * n + 3]) for n in range(4))
    in3 = tuple(turned(a) for a in in_new)
    return (block_out, input_grad, *ng3, *in3, *cv3, *hd3, *gg3, out_w, out_m, out_a)


def solution(mesh):
    act, vec, mat = P(None, "seq", None), P(), P(None, "head", None)
    weights = (vec, mat, mat, P(None, "head"), P("head"), P("head", None))
    outs = tuple(spec for spec in weights for _ in range(3))
    return jax.shard_map(
        shards,
        mesh=mesh,
        in_specs=(act, act, P(), *weights, *weights, *weights),
        out_specs=(act, act, *outs),
        check_vma=False,
    )
```

profile of v0, /device:TPU:0, one launch (start us, length us, event | category | flops | bytes accessed | tf_op | source)
XLA Modules:
  0.0 187.2 jit_solution(8432529621473702967)
XLA Ops:
  3.6 3.0 %collective-permute-start.19 = (bf16[144,768]{1,0:T(8,128)(2,1)S(1)}, bf16[144,768]{1,0:T(8,128)(2,1)S(1)}, u32[]{:S(2)}, u32[]{:S(2)}) collective-permute-start(bf16[144,768]{1,0:T(8,128)(2,1)S(1)} %get-tuple-element.212), channel_id=1, source_target_pairs={{0,4},{4,0},{8,12},{12,8},{16,20},{20,16},{24,28},{28,24},{1,5},{5... | collective-permute-start | bytes 663560 | tf_op jit(solution)/shard_map/ppermute | solution.py:882
  12.1 2.9 %collective-permute-done.20.refs_3_ = bf16[144,768]{1,0:T(8,128)(2,1)S(1)} collective-permute-done((bf16[144,768]{1,0:T(8,128)(2,1)S(1)}, bf16[144,768]{1,0:T(8,128)(2,1)S(1)}, u32[]{:S(2)}, u32[]{:S(2)}) %collective-permute-start.20) | collective-permute-done | bytes 221216 | tf_op jit(solution)/shard_map/ppermute | solution.py:882
  15.0 3.1 %collective-permute-done.21.refs_4_ = bf16[144,768]{1,0:T(8,128)(2,1)S(1)} collective-permute-done((bf16[144,768]{1,0:T(8,128)(2,1)S(1)}, bf16[144,768]{1,0:T(8,128)(2,1)S(1)}, u32[]{:S(2)}, u32[]{:S(2)}) %collective-permute-start.21) | collective-permute-done | bytes 221216 | tf_op jit(solution)/shard_map/ppermute | solution.py:882
  29.1 4.6 %first.1 = (bf16[1024,768]{1,0:T(8,128)(2,1)S(1)}, f32[1024,384]{1,0:T(8,128)S(1)}, f32[1024,128]{1,0:T(8,128)S(1)}, f32[8,1024]{1,0:T(8,128)S(1)}, f32[8,128]{1,0:T(8,128)}) custom-call(s32[11]{0:T(128)S(1)} %concatenate.3.refs_0_, bf16[4,128,768]{2,1,0:T(8,128)(2,1)S(1)} %get-tuple-element.216.refs_1_.refs_9_, ...), custom_call_target="tpu_custom_call" | custom-call | flops 805306368 | bytes 6782976 | tf_op jit(solution)/shard_map/first/pallas_call | solution.py:145
  33.7 5.7 %mix.1 = (f32[1024,384]{1,0:T(8,128)S(1)}, f32[1024,384]{1,0:T(8,128)S(1)}, f32[1024,384]{1,0:T(8,128)S(1)}, bf16[1024,384]{1,0:T(8,128)(2,1)S(1)}, f32[1024,64]...) custom-call(s32[11]{0:T(128)S(1)} %concatenate.3.refs_0_, ...), custom_call_target="tpu_custom_call" | custom-call | flops 1107296256 | bytes 12641024 | tf_op jit(solution)/shard_map/mix/pallas_call | solution.py:145
  43.4 4.2 %local.1 = (f32[1024,384]{1,0:T(8,128)S(1)}, f32[1024,384]{1,0:T(8,128)S(1)}, bf16[1024,768]{1,0:T(8,128)(2,1)S(1)}) custom-call(s32[11]{0:T(128)S(1)} %concatenate.3.refs_0_, bf16[1024,384]{1,0:T(8,128)(2,1)S(1)} %get-tuple-element.224.refs_1_, f32[1024,384]{1,0:T(8,128)S(1)} %get-tuple-element.225.refs_2_.refs_7_, ...), custom_call_target="tpu_custom_call" | custom-call | flops 1409286144 | bytes 11132928 | tf_op jit(solution)/shard_map/local/pallas_call | solution.py:145
  56.0 3.4 %ungate.1 = (f32[1024,384]{1,0:T(8,128)S(1)}, bf16[1024,384]{1,0:T(8,128)(2,1)S(1)}, bf16[1024,384]{1,0:T(8,128)(2,1)S(1)}, bf16[384,128]{1,0:T(8,128)(2,1)S(1)}...) custom-call(s32[11]{0:T(128)S(1)} %concatenate.3.refs_0_, ...), custom_call_target="tpu_custom_call" | custom-call | flops 704643072 | bytes 11079680 | tf_op jit(solution)/shard_map/ungate/pallas_call | solution.py:145
  64.2 2.9 %collective-permute-start.42 = (bf16[192,768]{1,0:T(8,128)(2,1)S(1)}, bf16[192,768]{1,0:T(8,128)(2,1)S(1)}, u32[]{:S(2)}, u32[]{:S(2)}) collective-permute-start(bf16[192,768]{1,0:T(8,128)(2,1)S(1)} %get-tuple-element.267), channel_id=1, source_target_pairs={{0,12},{4,8},{8,4},{12,0},{16,28},{20,24},{24,20},{28,16},{1,13},{... | collective-permute-start | bytes 884744 | tf_op jit(solution)/shard_map/ppermute | solution.py:882
  68.5 7.3 %inner.1 = (f32[1024,384]{1,0:T(8,128)S(1)}, f32[1024,128]{1,0:T(8,128)S(1)}, f32[1024,128]{1,0:T(8,128)S(1)}, f32[1024,128]{1,0:T(8,128)S(1)}, f32[4,384,128]{2,1,0:T(8,128)S(1)}) custom-call(s32[11]{0:T(128)S(1)} %concatenate.3.refs_0_, bf16[1024,384]{1,0:T(8,128)(2,1)S(1)} %get-tuple-element.224.refs_1_, ...), custom_call_target="tpu_custom_call" | custom-call | bytes 8257536 | tf_op jit(solution)/shard_map/inner/pallas_call | solution.py:145
  75.8 3.2 %collective-permute-done.35.refs_1_ = bf16[384,128]{1,0:T(8,128)(2,1)S(1)} collective-permute-done((bf16[384,128]{1,0:T(8,128)(2,1)S(1)}, bf16[384,128]{1,0:T(8,128)(2,1)S(1)}, u32[]{:S(2)}, u32[]{:S(2)}) %collective-permute-start.35) | collective-permute-done | bytes 98336 | tf_op jit(solution)/shard_map/ppermute | solution.py:882
  79.0 6.8 %back.1 = (f32[1024,384]{1,0:T(8,128)S(1)}, f32[8,384]{1,0:T(8,128)S(1)}, bf16[512,128]{1,0:T(8,128)(2,1)S(1)}, bf16[512,128]{1,0:T(8,128)(2,1)S(1)}, bf16[512,1...) custom-call(s32[11]{0:T(128)S(1)} %concatenate.3.refs_0_, ...), custom_call_target="tpu_custom_call" | custom-call | flops 402653184 | bytes 12201984 | tf_op jit(solution)/shard_map/back/pallas_call | solution.py:145
  86.0 3.4 %collective-permute-start.45 = (bf16[192,768]{1,0:T(8,128)(2,1)S(1)}, bf16[192,768]{1,0:T(8,128)(2,1)S(1)}, u32[]{:S(2)}, u32[]{:S(2)}) collective-permute-start(bf16[192,768]{1,0:T(8,128)(2,1)S(1)} %sum.6.refs_10_.refs_0_), channel_id=1, source_target_pairs={{0,16},{4,20},{8,24},{12,28},{16,0},{20,4},{24,8},{28,12},{1,17},{... | collective-permute-start | bytes 884744 | tf_op jit(solution)/shard_map/ppermute | solution.py:882
  91.4 5.4 %last_x.1 = (f32[1024,768]{1,0:T(8,128)S(1)}, f32[16,384]{1,0:T(8,128)S(1)}, f32[480,768]{1,0:T(8,128)S(1)}) custom-call(s32[11]{0:T(128)S(1)} %concatenate.3.refs_0_, f32[1024,384]{1,0:T(8,128)S(1)} %get-tuple-element.262.refs_1_.refs_2_, f32[1024,384]{1,0:T(8,128)S(1)} %get-tuple-element.262.refs_1_.refs_2_, ...), custom_call_target="tpu_custom_call" | custom-call | flops 2415919104 | bytes 13468416 | tf_op jit(solution)/shard_map/last_x/pallas_call | solution.py:145
  98.5 3.4 %collective-permute-done.45.refs_1_ = bf16[192,768]{1,0:T(8,128)(2,1)S(1)} collective-permute-done((bf16[192,768]{1,0:T(8,128)(2,1)S(1)}, bf16[192,768]{1,0:T(8,128)(2,1)S(1)}, u32[]{:S(2)}, u32[]{:S(2)}) %collective-permute-start.45) | collective-permute-done | bytes 294944 | tf_op jit(solution)/shard_map/ppermute | solution.py:882
  105.5 21.2 %conditional.3 = (bf16[64,768]{1,0:T(8,128)(2,1)}, bf16[64,768]{1,0:T(8,128)(2,1)}, bf16[64,768]{1,0:T(8,128)(2,1)}, bf16[64,768]{1,0:T(8,128)(2,1)}, bf16[120,7...) conditional(s32[]{:T(128)} %bitcast, () %tuple.34, (bf16[4,128,768]{2,1,0:T(8,128)(2,1)S(1)}, s32[11]{0:T(128)S(1)}, ...), branch_computations={%region_0.1_spmd, %region_1.2_spmd} | conditional | bytes 14143856 | solution.py:1000
  115.0 3.8 %collective-permute-done.2.refs_1_ = bf16[120,768]{1,0:T(8,128)(2,1)S(1)} collective-permute-done((bf16[120,768]{1,0:T(8,128)(2,1)S(1)}, bf16[120,768]{1,0:T(8,128)(2,1)S(1)}, u32[]{:S(2)}, u32[]{:S(2)}) %collective-permute-start.2) | collective-permute-done | bytes 184352 | tf_op jit(solution)/shard_map/cond/branch_1_fun/ppermute | solution.py:882
  127.9 14.6 %conditional.4 = (bf16[4,64,768]{2,1,0:T(8,128)(2,1)}, bf16[120,768]{1,0:T(8,128)(2,1)}) conditional(s32[]{:T(128)} %bitcast, () %tuple.33, (bf16[64,768]{1,0:T(8,128)(2,1)}, bf16[64,768]{1,0:T(8,128)(2,1)}, bf16[64,768]{1,0:T(8,128)(2,1)}, bf16[64,768]{1,0:T(8,128)(2,1)}, bf16[120,768]{1,0:T(8,128)(2,1)}) %tuple.36), branch_computations={%region_2.3_spmd, %region_3.4_spmd} | conditional | bytes 3256496 | solution.py:1000
  132.9 6.0 %collective-permute-done.10.refs_3_ = bf16[64,768]{1,0:T(8,128)(2,1)S(1)} collective-permute-done((bf16[64,768]{1,0:T(8,128)(2,1)}, bf16[64,768]{1,0:T(8,128)(2,1)S(1)}, u32[]{:S(2)}, u32[]{:S(2)}) %collective-permute-start.10) | collective-permute-done | bytes 98336 | tf_op jit(solution)/shard_map/cond/branch_1_fun/ppermute | solution.py:882
  142.5 14.5 %conditional.5 = (bf16[4,64,768]{2,1,0:T(8,128)(2,1)}, bf16[4,64,768]{2,1,0:T(8,128)(2,1)}, bf16[120,768]{1,0:T(8,128)(2,1)S(1)}, bf16[120,768]{1,0:T(8,128)(2,1...) conditional(s32[]{:T(128)} %bitcast, () %tuple.32, ...), branch_computations={%region_4.5_spmd, %region_5.6_spmd} | conditional | bytes 13594960 | solution.py:1000
  148.9 4.4 %home_out.1 = (bf16[4,256,768]{2,1,0:T(8,128)(2,1)}, f32[8,128]{1,0:T(8,128)}) custom-call(s32[11]{0:T(128)S(1)} %get-tuple-element.68.refs_0_, bf16[4,256,768]{2,1,0:T(8,128)(2,1)S(1)} %get-tuple-element.69.refs_1_, bf16[4,64,768]{2,1,0:T(8,128)(2,1)} %get-tuple-element.70.refs_2_, bf16[4,64,768]{2,1,0:T(8,128)(2,1)} %get-tuple-element.71.refs_3_, ...), custom_call_target="tpu_custom_call" | custom-call | bytes 4722688 | tf_op jit(solution)/shard_map/cond/branch_1_fun/home_out/pallas_call | solution.py:145
  153.9 3.0 %collective-permute-done.16 = bf16[120,768]{1,0:T(8,128)(2,1)} collective-permute-done((bf16[120,768]{1,0:T(8,128)(2,1)}, bf16[120,768]{1,0:T(8,128)(2,1)}, u32[]{:S(2)}, u32[]{:S(2)}) %collective-permute-start.16) | collective-permute-done | bytes 184352 | tf_op jit(solution)/shard_map/cond/branch_1_fun/ppermute | solution.py:882
  164.6 5.9 %update_b.1 = (f32[838,1,768]{2,1,0:T(1,128)}, f32[838,1,768]{2,1,0:T(1,128)}, f32[838,1,768]{2,1,0:T(1,128)}, f32[8,128]{1,0:T(8,128)}) custom-call(s32[11]{0:T(128)S(1)} %concatenate.3.refs_0_, bf16[120,768]{1,0:T(8,128)(2,1)} %copy-done.22, bf16[120,768]{1,0:T(8,128)(2,1)} %get-tuple-element.299.refs_2_, bf16[120,768]{1,0:T(8,128)(2,1)} %get-tuple-element.300.refs_3_, ...), custom_call_target="tpu_custom_call" | custom-call | bytes 16187392 | tf_op jit(solution)/shard_map/update_b/pallas_call | solution.py:145
  171.2 5.1 %home_grad.1 = (f32[4,256,768]{2,1,0:T(8,128)}, f32[8,128]{1,0:T(8,128)S(1)}) custom-call(s32[11]{0:T(128)S(1)} %concatenate.3.refs_0_, bf16[4,256,768]{2,1,0:T(8,128)(2,1)S(1)} %copy-done.21, bf16[4,256,768]{2,1,0:T(8,128)(2,1)S(1)} %copy-done, f32[8,768]{1,0:T(8,128)S(1)} %get-tuple-element.217.refs_3_.refs_11_.refs_7_.refs_10_.refs_14_, ...), custom_call_target="tpu_custom_call" | custom-call | bytes 7892992 | tf_op jit(solution)/shard_map/home_grad/pallas_call | solution.py:145
  177.3 8.3 %update_a.1 = (f32[384,768]{1,0:T(8,128)}, f32[384,768]{1,0:T(8,128)}, f32[384,768]{1,0:T(8,128)}, f32[838,1,768]{2,1,0:T(1,128)}, f32[838,1,768]{2,1,0:T(1,128)...) custom-call(s32[11]{0:T(128)S(1)} %concatenate.3.refs_0_, ...), custom_call_target="tpu_custom_call", output_to_operand_aliasing={{3}: (11, {}), {4}: (12, {}), {5}: (13, {})} | custom-call | bytes 31430656 | tf_op jit(solution)/shard_map/update_a/pallas_call | solution.py:145
  (174 shorter events, 89.8 us)
Async XLA Ops:
  18.7 10.4 %collective-permute-start.22 = (bf16[4,128,768]{2,1,0:T(8,128)(2,1)S(1)}, bf16[4,128,768]{2,1,0:T(8,128)(2,1)S(1)}, u32[]{:S(2)}, u32[]{:S(2)}) collective-permute-start(bf16[4,128,768]{2,1,0:T(8,128)(2,1)S(1)} %get-tuple-element.216.refs_1_.refs_9_), channel_id=1, source_target_pairs={{0,1},{1,0},{2,3},{3,2},{4,5},{5,4},{6,7},{7,6},{8,9},{9,8},{10,11... | collective-permute-start | bytes 2359304 | tf_op jit(solution)/shard_map/ppermute | solution.py:882
  24.1 15.3 %collective-permute-start.27 = (bf16[128,768]{1,0:T(8,128)(2,1)S(1)}, bf16[128,768]{1,0:T(8,128)(2,1)S(1)}, u32[]{:S(2)}, u32[]{:S(2)}) collective-permute-start(bf16[128,768]{1,0:T(8,128)(2,1)S(1)} %get-tuple-element.231), channel_id=1, source_target_pairs={{0,4},{4,0},{8,12},{12,8},{16,20},{20,16},{24,28},{28,24},{1,5},{5... | collective-permute-start | bytes 589832 | tf_op jit(solution)/shard_map/ppermute | solution.py:882
  25.7 13.7 %collective-permute-start.28 = (bf16[128,768]{1,0:T(8,128)(2,1)S(1)}, bf16[128,768]{1,0:T(8,128)(2,1)S(1)}, u32[]{:S(2)}, u32[]{:S(2)}) collective-permute-start(bf16[128,768]{1,0:T(8,128)(2,1)S(1)} %get-tuple-element.232), channel_id=1, source_target_pairs={{0,8},{4,12},{8,0},{12,4},{16,24},{20,28},{24,16},{28,20},{1,9},{5... | collective-permute-start | bytes 589832 | tf_op jit(solution)/shard_map/ppermute | solution.py:882
  27.3 12.2 %collective-permute-start.29 = (bf16[128,768]{1,0:T(8,128)(2,1)S(1)}, bf16[128,768]{1,0:T(8,128)(2,1)S(1)}, u32[]{:S(2)}, u32[]{:S(2)}) collective-permute-start(bf16[128,768]{1,0:T(8,128)(2,1)S(1)} %get-tuple-element.233), channel_id=1, source_target_pairs={{0,12},{4,8},{8,4},{12,0},{16,28},{20,24},{24,20},{28,16},{1,13},{... | collective-permute-start | bytes 589832 | tf_op jit(solution)/shard_map/ppermute | solution.py:882
  62.6 28.7 %collective-permute-start.43 = (bf16[4,64,768]{2,1,0:T(8,128)(2,1)S(1)}, bf16[4,64,768]{2,1,0:T(8,128)(2,1)S(1)}, u32[]{:S(2)}, u32[]{:S(2)}) collective-permute-start(bf16[4,64,768]{2,1,0:T(8,128)(2,1)S(1)} %get-tuple-element.249.refs_9_), channel_id=1, source_target_pairs={{0,2},{1,3},{2,0},{3,1},{4,6},{5,7},{6,4},{7,5},{8,10},{9,11},{10,... | collective-permute-start | bytes 1179656 | tf_op jit(solution)/shard_map/ppermute | solution.py:882
  63.6 22.2 %collective-permute-start.40 = (bf16[192,768]{1,0:T(8,128)(2,1)S(1)}, bf16[192,768]{1,0:T(8,128)(2,1)S(1)}, u32[]{:S(2)}, u32[]{:S(2)}) collective-permute-start(bf16[192,768]{1,0:T(8,128)(2,1)S(1)} %get-tuple-element.265), channel_id=1, source_target_pairs={{0,4},{4,0},{8,12},{12,8},{16,20},{20,16},{24,28},{28,24},{1,5},{5... | collective-permute-start | bytes 884744 | tf_op jit(solution)/shard_map/ppermute | solution.py:882
  64.1 21.7 %collective-permute-start.41 = (bf16[192,768]{1,0:T(8,128)(2,1)S(1)}, bf16[192,768]{1,0:T(8,128)(2,1)S(1)}, u32[]{:S(2)}, u32[]{:S(2)}) collective-permute-start(bf16[192,768]{1,0:T(8,128)(2,1)S(1)} %get-tuple-element.266), channel_id=1, source_target_pairs={{0,8},{4,12},{8,0},{12,4},{16,24},{20,28},{24,16},{28,20},{1,9},{5... | collective-permute-start | bytes 884744 | tf_op jit(solution)/shard_map/ppermute | solution.py:882
  64.2 21.6 %collective-permute-start.42 = (bf16[192,768]{1,0:T(8,128)(2,1)S(1)}, bf16[192,768]{1,0:T(8,128)(2,1)S(1)}, u32[]{:S(2)}, u32[]{:S(2)}) collective-permute-start(bf16[192,768]{1,0:T(8,128)(2,1)S(1)} %get-tuple-element.267), channel_id=1, source_target_pairs={{0,12},{4,8},{8,4},{12,0},{16,28},{20,24},{24,20},{28,16},{1,13},{... | collective-permute-start | bytes 884744 | tf_op jit(solution)/shard_map/ppermute | solution.py:882
  67.1 11.9 %collective-permute-start.35 = (bf16[384,128]{1,0:T(8,128)(2,1)S(1)}, bf16[384,128]{1,0:T(8,128)(2,1)S(1)}, u32[]{:S(2)}, u32[]{:S(2)}) collective-permute-start(bf16[384,128]{1,0:T(8,128)(2,1)S(1)} %get-tuple-element.241), channel_id=1, source_target_pairs={{0,16},{4,20},{8,24},{12,28},{16,0},{20,4},{24,8},{28,12},{1,17},{... | collective-permute-start | bytes 294920 | tf_op jit(solution)/shard_map/ppermute | solution.py:882
  86.0 16.0 %collective-permute-start.45 = (bf16[192,768]{1,0:T(8,128)(2,1)S(1)}, bf16[192,768]{1,0:T(8,128)(2,1)S(1)}, u32[]{:S(2)}, u32[]{:S(2)}) collective-permute-start(bf16[192,768]{1,0:T(8,128)(2,1)S(1)} %sum.6.refs_10_.refs_0_), channel_id=1, source_target_pairs={{0,16},{4,20},{8,24},{12,28},{16,0},{20,4},{24,8},{28,12},{1,17},{... | collective-permute-start | bytes 884744 | tf_op jit(solution)/shard_map/ppermute | solution.py:882
  108.8 11.2 %collective-permute-start.1 = (bf16[4,64,768]{2,1,0:T(8,128)(2,1)S(1)}, bf16[4,64,768]{2,1,0:T(8,128)(2,1)S(1)}, u32[]{:S(2)}, u32[]{:S(2)}) collective-permute-start(bf16[4,64,768]{2,1,0:T(8,128)(2,1)S(1)} %get-tuple-element.48), channel_id=1, source_target_pairs={{0,2},{1,3},{2,0},{3,1},{4,6},{5,7},{6,4},{7,5},{8,10},{9,11},{10,... | collective-permute-start | bytes 1179656 | tf_op jit(solution)/shard_map/cond/branch_1_fun/ppermute | solution.py:882
  111.5 11.0 %collective-permute-start.3 = (bf16[120,768]{1,0:T(8,128)(2,1)S(1)}, bf16[120,768]{1,0:T(8,128)(2,1)S(1)}, u32[]{:S(2)}, u32[]{:S(2)}) collective-permute-start(bf16[120,768]{1,0:T(8,128)(2,1)S(1)} %get-tuple-element.55), channel_id=1, source_target_pairs={{0,8},{4,12},{8,0},{12,4},{16,24},{20,28},{24,16},{28,20},{1,9},{5... | collective-permute-start | bytes 552968 | tf_op jit(solution)/shard_map/cond/branch_1_fun/ppermute | solution.py:882
  112.0 10.7 %collective-permute-start.4 = (bf16[120,768]{1,0:T(8,128)(2,1)S(1)}, bf16[120,768]{1,0:T(8,128)(2,1)S(1)}, u32[]{:S(2)}, u32[]{:S(2)}) collective-permute-start(bf16[120,768]{1,0:T(8,128)(2,1)S(1)} %get-tuple-element.56), channel_id=1, source_target_pairs={{0,12},{4,8},{8,4},{12,0},{16,28},{20,24},{24,20},{28,16},{1,13},{... | collective-permute-start | bytes 552968 | tf_op jit(solution)/shard_map/cond/branch_1_fun/ppermute | solution.py:882
  113.5 9.9 %collective-permute-start.5 = (bf16[64,768]{1,0:T(8,128)(2,1)S(1)}, bf16[64,768]{1,0:T(8,128)(2,1)S(1)}, u32[]{:S(2)}, u32[]{:S(2)}) collective-permute-start(bf16[64,768]{1,0:T(8,128)(2,1)S(1)} %get-tuple-element.58), channel_id=1, source_target_pairs={{0,4},{4,0},{8,12},{12,8},{16,20},{20,16},{24,28},{28,24},{1,5},{5... | collective-permute-start | bytes 294920 | tf_op jit(solution)/shard_map/cond/branch_1_fun/ppermute | solution.py:882
  126.7 15.8 %collective-permute-start.46 = (bf16[4,64,768]{2,1,0:T(8,128)(2,1)}, bf16[4,64,768]{2,1,0:T(8,128)(2,1)}, u32[]{:S(2)}, u32[]{:S(2)}) collective-permute-start(bf16[4,64,768]{2,1,0:T(8,128)(2,1)} %get-tuple-element.294), channel_id=1, source_target_pairs={{0,2},{1,3},{2,0},{3,1},{4,6},{5,7},{6,4},{7,5},{8,10},{9,11},{10,... | collective-permute-start | bytes 1179656 | tf_op jit(solution)/shard_map/ppermute | solution.py:882
  127.9 13.0 %collective-permute-start.11 = (bf16[120,768]{1,0:T(8,128)(2,1)}, bf16[120,768]{1,0:T(8,128)(2,1)S(1)}, u32[]{:S(2)}, u32[]{:S(2)}) collective-permute-start(bf16[120,768]{1,0:T(8,128)(2,1)} %get-tuple-element.65.refs_0_), channel_id=1, source_target_pairs={{0,16},{4,20},{8,24},{12,28},{16,0},{20,4},{24,8},{28,12},{1,17},{... | collective-permute-start | bytes 552968 | tf_op jit(solution)/shard_map/cond/branch_1_fun/ppermute | solution.py:882
  143.0 13.9 %collective-permute-start.12 = (bf16[4,64,768]{2,1,0:T(8,128)(2,1)}, bf16[4,64,768]{2,1,0:T(8,128)(2,1)}, u32[]{:S(2)}, u32[]{:S(2)}) collective-permute-start(bf16[4,64,768]{2,1,0:T(8,128)(2,1)} %get-tuple-element.66), channel_id=1, source_target_pairs={{0,2},{1,3},{2,0},{3,1},{4,6},{5,7},{6,4},{7,5},{8,10},{9,11},{10,... | collective-permute-start | bytes 1179656 | tf_op jit(solution)/shard_map/cond/branch_1_fun/ppermute | solution.py:882
  144.4 12.5 %collective-permute-start.13 = (bf16[4,64,768]{2,1,0:T(8,128)(2,1)}, bf16[4,64,768]{2,1,0:T(8,128)(2,1)}, u32[]{:S(2)}, u32[]{:S(2)}) collective-permute-start(bf16[4,64,768]{2,1,0:T(8,128)(2,1)} %get-tuple-element.66), channel_id=1, source_target_pairs={{0,1},{1,0},{2,3},{3,2},{4,5},{5,4},{6,7},{7,6},{8,9},{9,8},{10,11... | collective-permute-start | bytes 1179656 | tf_op jit(solution)/shard_map/cond/branch_1_fun/ppermute | solution.py:882
  146.2 10.8 %collective-permute-start.16 = (bf16[120,768]{1,0:T(8,128)(2,1)}, bf16[120,768]{1,0:T(8,128)(2,1)}, u32[]{:S(2)}, u32[]{:S(2)}) collective-permute-start(bf16[120,768]{1,0:T(8,128)(2,1)} %get-tuple-element.354), channel_id=1, source_target_pairs={{0,12},{4,8},{8,4},{12,0},{16,28},{20,24},{24,20},{28,16},{1,13},{... | collective-permute-start | bytes 552968 | tf_op jit(solution)/shard_map/cond/branch_1_fun/ppermute | solution.py:882
  156.9 13.6 %collective-permute-start.47 = (bf16[4,64,768]{2,1,0:T(8,128)(2,1)}, bf16[4,64,768]{2,1,0:T(8,128)(2,1)S(1)}, u32[]{:S(2)}, u32[]{:S(2)}) collective-permute-start(bf16[4,64,768]{2,1,0:T(8,128)(2,1)} %get-tuple-element.296.refs_5_), channel_id=1, source_target_pairs={{0,1},{1,0},{2,3},{3,2},{4,5},{5,4},{6,7},{7,6},{8,9},{9,8},{10,11... | collective-permute-start | bytes 1179656 | tf_op jit(solution)/shard_map/ppermute | solution.py:882
  157.0 19.3 %collective-permute-start.50 = (bf16[192,768]{1,0:T(8,128)(2,1)S(1)}, bf16[192,768]{1,0:T(8,128)(2,1)S(1)}, u32[]{:S(2)}, u32[]{:S(2)}) collective-permute-start(bf16[192,768]{1,0:T(8,128)(2,1)S(1)} %sum.7.refs_16_.refs_1_), channel_id=1, source_target_pairs={{0,4},{4,0},{8,12},{12,8},{16,20},{20,16},{24,28},{28,24},{1,5},{5... | collective-permute-start | bytes 884744 | tf_op jit(solution)/shard_map/ppermute | solution.py:882
  158.8 17.6 %collective-permute-start.51 = (bf16[192,768]{1,0:T(8,128)(2,1)S(1)}, bf16[192,768]{1,0:T(8,128)(2,1)S(1)}, u32[]{:S(2)}, u32[]{:S(2)}) collective-permute-start(bf16[192,768]{1,0:T(8,128)(2,1)S(1)} %sum.7.refs_16_.refs_1_), channel_id=1, source_target_pairs={{0,8},{4,12},{8,0},{12,4},{16,24},{20,28},{24,16},{28,20},{1,9},{5... | collective-permute-start | bytes 884744 | tf_op jit(solution)/shard_map/ppermute | solution.py:882
  159.1 17.3 %collective-permute-start.52 = (bf16[192,768]{1,0:T(8,128)(2,1)S(1)}, bf16[192,768]{1,0:T(8,128)(2,1)S(1)}, u32[]{:S(2)}, u32[]{:S(2)}) collective-permute-start(bf16[192,768]{1,0:T(8,128)(2,1)S(1)} %sum.7.refs_16_.refs_1_), channel_id=1, source_target_pairs={{0,12},{4,8},{8,4},{12,0},{16,28},{20,24},{24,20},{28,16},{1,13},{... | collective-permute-start | bytes 884744 | tf_op jit(solution)/shard_map/ppermute | solution.py:882
  163.5 22.1 %collective-permute-start.49 = (f32[8,768]{1,0:T(8,128)S(1)}, f32[8,768]{1,0:T(8,128)S(1)}, u32[]{:S(2)}, u32[]{:S(2)}) collective-permute-start(f32[8,768]{1,0:T(8,128)S(1)} %add_small.1.refs_8_.refs_1_), channel_id=1, source_target_pairs={{0,2},{1,3},{2,0},{3,1},{4,6},{5,7},{6,4},{7,5},{8,10},{9,11},{10,... | collective-permute-start | bytes 73736 | tf_op jit(solution)/shard_map/ppermute | solution.py:882
  (56 other events, 388.4 us)
where the time goes:
time: 188 us; the launch traced here: 187 us
  Pallas kernels  84.8 us (45%)
  starting transfers between devices  56 us (30%)
  waiting for transfers between devices  40.9 us (22%)
  local copies, waits for them, and re-layouts  4.03 us (2%)
    pallas_call x33, Pallas kernels, call(): pl.pallas_call(body, grid_spec=spec, out_shape=outs, compiler_params=pltp...  84.8 us
    ppermute x53, starting transfers between devices, trade(): return lambda array: lax.ppermute(array, axis, pairs)  56 us
    ppermute x53, waiting for transfers between devices, trade(): return lambda array: lax.ppermute(array, axis, pairs)  40.9 us
  transfers between devices with their start and end apart: 53, of which 21 were waited for; matrix products, arithmetic and copies ran while one was open for 1% of the time, Pallas kernels for 38%

commit v1 on v0

--- a/solution.py
+++ b/solution.py
@@ -112,11 +112,23 @@
 
         def kernel(*refs):
             at = refs[:pre]
-            for i in range(GRP):
+
+            def step(i):
                 views = [part_of(r, c, i, at) for r, c in zip(refs[pre:used], cuts)]
                 STEP.append(i)
                 plain(*at, *views, *refs[used:])
                 STEP.pop()
+
+            def two_steps(k, carry):
+                step(2 * k)
+                step(2 * k + 1)
+                return carry
+
+            if name in BY_TWOS:
+                lax.fori_loop(0, GRP // 2, two_steps, 0)
+            else:
+                for i in range(GRP):
+                    step(i)
 
         grid = (1,)
         in_specs, out_specs = [whole(a.shape) for a in ins], [whole(a.shape) for a in outs]
@@ -156,7 +168,8 @@
 
 
 STEP = []
-STREAMED = ("home_out", "home_grad", "split", "gate", "inner", "edge", "last_x", "local", "back", )
+BY_TWOS = ("inner", )
+STREAMED = ("home_out", "home_grad", "split", "gate", "edge", "last_x", )
 
 
 def step_now():
@@ -500,7 +513,8 @@
     scores = nt(cc, bb)
     d_scores = jnp.zeros((BLK, BLK), F32)
     d_cum = jnp.zeros((BLK, LANES), F32)
-    columns = []
+    columns = jnp.zeros((8, BLK), F32)
+    row8 = iota((8, BLK), 0)
     dyv = dy[...]
     for p in range(NH // 2):
         x = xdt[:, LANES * p : LANES * (p + 1)]
@@ -512,12 +526,12 @@
             d_h = d * lane_mask(q)
             d_spans = nt(d_h, x) * spans
             d_scores = d_scores + d_spans
-            both = d_spans * scores
-            d_cum = d_cum + jnp.where(lane == h, jnp.sum(both, axis=1, keepdims=True), 0.0)
-            columns.append(jnp.sum(both, axis=0, keepdims=True))
+            both = (d_spans * scores).astype(BF16)
+            d_cum = d_cum + nn(both, (lane == h).astype(BF16))
+            columns = columns + nn((row8 == h).astype(BF16), both)
             total = total + tn((spans * scores).astype(BF16), d_h)
         dxi_ref[:, LANES * p : LANES * (p + 1)] = total
-    columns = jnp.concatenate(columns + [jnp.zeros((LANES - NH, BLK), F32)], axis=0)
+    columns = jnp.concatenate([columns, jnp.zeros((LANES - 8, BLK), F32)], axis=0)
     d_cum = d_cum - jnp.transpose(columns)
     low_scores = d_scores.astype(BF16)
     c_exp = jnp.exp(jnp.where(lane < 8, packed, 0.0))
@@ -769,7 +783,7 @@
     return (weight_new, moment_new, average_new)
 
 
-def stepped(grad_of, weights, outs, blocks, buffers, sems, rate):
+def stepped(grad, grad_at, weights, outs, blocks, buffers, sems, rate):
     ins, done = buffers[:3], buffers[3:]
 
     def reads(n):
@@ -796,10 +810,17 @@
     for n, (start, size) in enumerate(blocks):
         for copy in reads(n):
             copy.wait()
-        here = pl.ds(start, size)
-        new = advance(ins[0][here, :], grad_of(n), ins[1][here, :], ins[2][here, :], rate)
-        for buf, value in zip(done, new):
-            buf[here, :] = value
+        cut = 16 if size % 16 == 0 else size
+
+        def some(k, carry):
+            here = pl.ds(pl.multiple_of(start + k * cut, 8), cut)
+            there = pl.ds(pl.multiple_of(grad_at(n) + k * cut, 8), cut)
+            new = advance(ins[0][here, :], grad[there, :], ins[1][here, :], ins[2][here, :], rate)
+            for buf, value in zip(done, new):
+                buf[here, :] = value
+            return carry
+
+        lax.fori_loop(0, size // cut, some, 0)
         for copy in writes(n):
             copy.start()
     for n in range(len(blocks)):
@@ -818,7 +839,7 @@
     for b, ref in enumerate((g0, g1, g2, g3)):
         grad[pl.ds(pl.multiple_of((at[0] ^ b) * SEG1, SEG1), SEG1), :] = ref[0:SEG1, :].astype(F32)
     stepped(
-        lambda n: grad[96 * n : 96 * (n + 1), :], (wi, mi, ai), (wo, mo, ao), Z_BLOCKS,
+        grad, lambda n: 96 * n, (wi, mi, ai), (wo, mo, ao), Z_BLOCKS,
         (b0, b1, b2, b3, b4, b5), sems, rate_in,
     )
     w_ref[...], m_ref[...], a_ref[...] = advance(w[...], grad[ZW:, :], m[...], a[...], rate)
@@ -832,7 +853,7 @@
         start = pl.multiple_of((at[0] ^ b) * SEG2, 8)
         grad[pl.ds(start, SEG2), :] = ref[...].astype(F32)
     stepped(
-        lambda n: grad[96 * n : min(96 * (n + 1), COLS - ZW), :], (wi, mi, ai), (wo, mo, ao), X_BLOCKS,
+        grad, lambda n: 96 * n, (wi, mi, ai), (wo, mo, ao), X_BLOCKS,
         (b0, b1, b2, b3, b4, b5), sems, rate,
     )
 
@@ -1103,7 +1124,6 @@
     )
     quarters = quarter_add(keep2, other2, (g_head,))
     one, joint = whole((SEG1, D)), whole((SEG1 + QUART, D))
-    mine1 = add_rows(SEG1, [grads1[0], *got1], (g_head,))
 
     def after_rows(width):
         last = TOK // 8 - 1
@@ -1119,7 +1139,7 @@
         [rows(ZW), after_rows(ZW), rows(ZW), whole((5, 1, 448)), rows(ZW), rows(LANES),
          rows(D), whole((2 * ZW, D)), whole((LANES, D))],
         [sds((TOK, D)), sds((END, ZW)), sds((final, D))], [rows(D), whole((END, ZW)), whole((final, D))],
-        scratch=[pltpu.VMEM((BLK + 8, ZW), F32)], prefetch=at, flops=4 * TOK * D * 2 * ZW, after=(mine1, quarters[0]),
+        scratch=[pltpu.VMEM((BLK + 8, ZW), F32)], prefetch=at, flops=4 * TOK * D * 2 * ZW, after=(quarters[0],),
     )
     dpo, halo_o = call(
         edge_kernel, "edge", (GRP,), (dbc[0], *bc_got, po, halo_x),
@@ -1127,7 +1147,7 @@
         [sds((TOK, 2 * SW)), sds((8, ZW + LANES))], [rows(2 * SW), whole((8, ZW + LANES))], after=(acc,),
     )
     halo_o = moved(halo_o, -GRP)
-    total1 = across_groups(mine1, SEG1, (halo_o,))
+    mine1 = add_rows(SEG1, [grads1[0], *got1], (halo_o,))
     keep_b, send_b, *grads2 = call(
         last_o_kernel, "last_o", (GRP,),
         (dpo, dpo, halo_o, mo, conv_params, nrm, w, w, pb, vecs, g_gate, g_head, acc, end, mx),
@@ -1137,16 +1157,17 @@
         [sds((GRP, HALF, D), BF16)] * 2 + [sds((SEG2, D), BF16)] * 4,
         [half_rows] * 2 + [whole((SEG2, D))] * 4,
         scratch=[pltpu.VMEM((BLK + 8, 2 * SW), F32), pltpu.VMEM((final, D), F32), pltpu.VMEM((BLK, D), F32)],
-        prefetch=at, flops=4 * TOK * D * 2 * SW, after=(total1,),
+        prefetch=at, flops=4 * TOK * D * 2 * SW, after=(mine1,),
     )
 
     def finish():
         keep3, send3 = split_both(at, keep_b, trade("head", 1)(send_b))
         quarters_b = quarter_add(keep3, trade("head", 2)(send3))
         mine2 = group_sum(grads2, SEG2, (quarters_b[0],))
-        return quarters_b, mine2, quarter_home(quarters, (mine2,))
-
-    quarters_b, mine2, own_out = apart(finish)
+        own = quarter_home(quarters, (mine2,))
+        return quarters_b, mine2, own, across_groups(mine1, SEG1, (own,))
+
+    quarters_b, mine2, own_out, total1 = apart(finish)
     x_out = trade("head", 2)(own_out)
     root = math.sqrt(TOK * lax.axis_size("seq"))
     mat = whole((ZW, D))

time: 188 us -> 185 us (0.984)
  Pallas kernels: 84.8 us -> 81.5 us
    pallas_call x33, Pallas kernels: 84.8 us -> 81.5 us  [call(): pl.pallas_call(body, grid_spec=spec, out_shape=outs, compiler_params=pltp...]
  transfers between devices with their start and end apart: 53 -> 53, of which waited for: 21 -> 20; matrix products, arithmetic and copies ran while one was open for 1% -> 1% of each run, Pallas kernels for 38% -> 37%
where the time goes in v1:
time: 185 us; the launch traced here: 184 us
  Pallas kernels  81.5 us (44%)
  starting transfers between devices  54.7 us (30%)
  waiting for transfers between devices  41.7 us (23%)
  local copies, waits for them, and re-layouts  4.63 us (3%)
    pallas_call x33, Pallas kernels, call(): pl.pallas_call(body, grid_spec=spec, out_shape=outs, compiler_params=pltp...  81.5 us
    ppermute x53, starting transfers between devices, trade(): return lambda array: lax.ppermute(array, axis, pairs)  54.7 us
    ppermute x53, waiting for transfers between devices, trade(): return lambda array: lax.ppermute(array, axis, pairs)  41.7 us
  transfers between devices with their start and end apart: 53, of which 20 were waited for; matrix products, arithmetic and copies ran while one was open for 1% of the time, Pallas kernels for 37%

profile of v1, /device:TPU:0, one launch (start us, length us, event | category | flops | bytes accessed | tf_op | source)
XLA Modules:
  0.0 184.1 jit_solution(2632912819441419399)
XLA Ops:
  3.6 3.0 %collective-permute-start.20 = (bf16[144,768]{1,0:T(8,128)(2,1)S(1)}, bf16[144,768]{1,0:T(8,128)(2,1)S(1)}, u32[]{:S(2)}, u32[]{:S(2)}) collective-permute-start(bf16[144,768]{1,0:T(8,128)(2,1)S(1)} %get-tuple-element.216), channel_id=1, source_target_pairs={{0,4},{4,0},{8,12},{12,8},{16,20},{20,16},{24,28},{28,24},{1,5},{5... | collective-permute-start | bytes 663560 | tf_op jit(solution)/shard_map/ppermute | solution.py:903
  12.1 2.9 %collective-permute-done.21.refs_3_ = bf16[144,768]{1,0:T(8,128)(2,1)S(1)} collective-permute-done((bf16[144,768]{1,0:T(8,128)(2,1)S(1)}, bf16[144,768]{1,0:T(8,128)(2,1)S(1)}, u32[]{:S(2)}, u32[]{:S(2)}) %collective-permute-start.21) | collective-permute-done | bytes 221216 | tf_op jit(solution)/shard_map/ppermute | solution.py:903
  15.0 3.1 %collective-permute-done.22.refs_4_ = bf16[144,768]{1,0:T(8,128)(2,1)S(1)} collective-permute-done((bf16[144,768]{1,0:T(8,128)(2,1)S(1)}, bf16[144,768]{1,0:T(8,128)(2,1)S(1)}, u32[]{:S(2)}, u32[]{:S(2)}) %collective-permute-start.22) | collective-permute-done | bytes 221216 | tf_op jit(solution)/shard_map/ppermute | solution.py:903
  29.1 4.6 %first.1 = (bf16[1024,768]{1,0:T(8,128)(2,1)S(1)}, f32[1024,384]{1,0:T(8,128)S(1)}, f32[1024,128]{1,0:T(8,128)S(1)}, f32[8,1024]{1,0:T(8,128)S(1)}, f32[8,128]{1,0:T(8,128)}) custom-call(s32[11]{0:T(128)S(1)} %concatenate.3.refs_0_, bf16[4,128,768]{2,1,0:T(8,128)(2,1)S(1)} %get-tuple-element.220.refs_1_.refs_9_, ...), custom_call_target="tpu_custom_call" | custom-call | flops 805306368 | bytes 6782976 | tf_op jit(solution)/shard_map/first/pallas_call | solution.py:157
  33.7 5.8 %mix.1 = (f32[1024,384]{1,0:T(8,128)S(1)}, f32[1024,384]{1,0:T(8,128)S(1)}, f32[1024,384]{1,0:T(8,128)S(1)}, bf16[1024,384]{1,0:T(8,128)(2,1)S(1)}, f32[1024,64]...) custom-call(s32[11]{0:T(128)S(1)} %concatenate.3.refs_0_, ...), custom_call_target="tpu_custom_call" | custom-call | flops 1107296256 | bytes 12641024 | tf_op jit(solution)/shard_map/mix/pallas_call | solution.py:157
  40.5 2.9 %collective-permute-start.32 = (bf16[384,128]{1,0:T(8,128)(2,1)S(1)}, bf16[384,128]{1,0:T(8,128)(2,1)S(1)}, u32[]{:S(2)}, u32[]{:S(2)}) collective-permute-start(bf16[384,128]{1,0:T(8,128)(2,1)S(1)} %get-tuple-element.238.refs_5_), channel_id=1, source_target_pairs={{0,16},{4,20},{8,24},{12,28},{16,0},{20,4},{24,8},{28,12},{1,17},{... | collective-permute-start | bytes 294920 | tf_op jit(solution)/shard_map/ppermute | solution.py:903
  43.4 3.3 %local.1 = (f32[1024,384]{1,0:T(8,128)S(1)}, f32[1024,384]{1,0:T(8,128)S(1)}, bf16[1024,768]{1,0:T(8,128)(2,1)S(1)}) custom-call(s32[11]{0:T(128)S(1)} %concatenate.3.refs_0_, bf16[1024,384]{1,0:T(8,128)(2,1)S(1)} %get-tuple-element.228.refs_1_, f32[1024,384]{1,0:T(8,128)S(1)} %get-tuple-element.229.refs_2_.refs_7_, ...), custom_call_target="tpu_custom_call" | custom-call | flops 1409286144 | bytes 11132928 | tf_op jit(solution)/shard_map/local/pallas_call | solution.py:157
  56.2 3.4 %ungate.1 = (f32[1024,384]{1,0:T(8,128)S(1)}, bf16[1024,384]{1,0:T(8,128)(2,1)S(1)}, bf16[1024,384]{1,0:T(8,128)(2,1)S(1)}, bf16[384,128]{1,0:T(8,128)(2,1)S(1)}...) custom-call(s32[11]{0:T(128)S(1)} %concatenate.3.refs_0_, ...), custom_call_target="tpu_custom_call" | custom-call | flops 704643072 | bytes 11079680 | tf_op jit(solution)/shard_map/ungate/pallas_call | solution.py:157
  64.4 6.8 %inner.1 = (f32[1024,384]{1,0:T(8,128)S(1)}, f32[1024,128]{1,0:T(8,128)S(1)}, f32[1024,128]{1,0:T(8,128)S(1)}, f32[1024,128]{1,0:T(8,128)S(1)}, f32[4,384,128]{2,1,0:T(8,128)S(1)}) custom-call(s32[11]{0:T(128)S(1)} %concatenate.3.refs_0_, bf16[1024,384]{1,0:T(8,128)(2,1)S(1)} %get-tuple-element.228.refs_1_, ...), custom_call_target="tpu_custom_call" | custom-call | bytes 8257536 | tf_op jit(solution)/shard_map/inner/pallas_call | solution.py:157
  71.5 5.8 %back.1 = (f32[1024,384]{1,0:T(8,128)S(1)}, f32[8,384]{1,0:T(8,128)S(1)}, bf16[512,128]{1,0:T(8,128)(2,1)S(1)}, bf16[512,128]{1,0:T(8,128)(2,1)S(1)}, bf16[512,1...) custom-call(s32[11]{0:T(128)S(1)} %concatenate.3.refs_0_, ...), custom_call_target="tpu_custom_call" | custom-call | flops 402653184 | bytes 12201984 | tf_op jit(solution)/shard_map/back/pallas_call | solution.py:157
  82.9 5.3 %last_x.1 = (f32[1024,768]{1,0:T(8,128)S(1)}, f32[16,384]{1,0:T(8,128)S(1)}, f32[480,768]{1,0:T(8,128)S(1)}) custom-call(s32[11]{0:T(128)S(1)} %concatenate.3.refs_0_, f32[1024,384]{1,0:T(8,128)S(1)} %get-tuple-element.266.refs_1_.refs_2_, f32[1024,384]{1,0:T(8,128)S(1)} %get-tuple-element.266.refs_1_.refs_2_, ...), custom_call_target="tpu_custom_call" | custom-call | flops 2415919104 | bytes 13468416 | tf_op jit(solution)/shard_map/last_x/pallas_call | solution.py:157
  90.6 4.9 %collective-permute-done.45.refs_3_ = bf16[192,768]{1,0:T(8,128)(2,1)S(1)} collective-permute-done((bf16[192,768]{1,0:T(8,128)(2,1)S(1)}, bf16[192,768]{1,0:T(8,128)(2,1)S(1)}, u32[]{:S(2)}, u32[]{:S(2)}) %collective-permute-start.45) | collective-permute-done | bytes 294944 | tf_op jit(solution)/shard_map/ppermute | solution.py:903
  97.8 27.7 %conditional.3 = (bf16[64,768]{1,0:T(8,128)(2,1)}, bf16[64,768]{1,0:T(8,128)(2,1)S(1)}, bf16[64,768]{1,0:T(8,128)(2,1)S(1)}, bf16[64,768]{1,0:T(8,128)(2,1)}, bf...) conditional(s32[]{:T(128)} %bitcast, () %tuple.34, ...), branch_computations={%region_0.1_spmd, %region_1.2_spmd} | conditional | bytes 16208288 | solution.py:1021
  107.4 3.2 %collective-permute-done.2.refs_1_ = bf16[120,768]{1,0:T(8,128)(2,1)S(1)} collective-permute-done((bf16[120,768]{1,0:T(8,128)(2,1)S(1)}, bf16[120,768]{1,0:T(8,128)(2,1)S(1)}, u32[]{:S(2)}, u32[]{:S(2)}) %collective-permute-start.2) | collective-permute-done | bytes 184352 | tf_op jit(solution)/shard_map/cond/branch_1_fun/ppermute | solution.py:903
  112.1 3.2 %collective-permute-done.3.refs_2_ = bf16[120,768]{1,0:T(8,128)(2,1)S(1)} collective-permute-done((bf16[120,768]{1,0:T(8,128)(2,1)S(1)}, bf16[120,768]{1,0:T(8,128)(2,1)S(1)}, u32[]{:S(2)}, u32[]{:S(2)}) %collective-permute-start.3) | collective-permute-done | bytes 184352 | tf_op jit(solution)/shard_map/cond/branch_1_fun/ppermute | solution.py:903
  126.4 13.3 %conditional.4 = (bf16[4,64,768]{2,1,0:T(8,128)(2,1)}, bf16[120,768]{1,0:T(8,128)(2,1)S(1)}) conditional(s32[]{:T(128)} %bitcast, () %tuple.33, (bf16[64,768]{1,0:T(8,128)(2,1)S(1)}, bf16[64,768]{1,0:T(8,128)(2,1)S(1)}, bf16[64,768]{1,0:T(8,128)(2,1)}, bf16[64,768]{1,0:T(8,128)(2,1)}, bf16[120,768]{1,0:T(8,128)(2,1)}) %tuple.36), branch_computations={%region_2.3_spmd, %region_3.4_spmd} | conditional | bytes 3256496 | solution.py:1021
  130.8 3.3 %collective-permute-done.10.refs_2_ = bf16[64,768]{1,0:T(8,128)(2,1)S(1)} collective-permute-done((bf16[64,768]{1,0:T(8,128)(2,1)S(1)}, bf16[64,768]{1,0:T(8,128)(2,1)S(1)}, u32[]{:S(2)}, u32[]{:S(2)}) %collective-permute-start.10) | collective-permute-done | bytes 98336 | tf_op jit(solution)/shard_map/cond/branch_1_fun/ppermute | solution.py:903
  134.1 2.9 %collective-permute-done.11.refs_3_ = bf16[64,768]{1,0:T(8,128)(2,1)S(1)} collective-permute-done((bf16[64,768]{1,0:T(8,128)(2,1)}, bf16[64,768]{1,0:T(8,128)(2,1)S(1)}, u32[]{:S(2)}, u32[]{:S(2)}) %collective-permute-start.11) | collective-permute-done | bytes 98336 | tf_op jit(solution)/shard_map/cond/branch_1_fun/ppermute | solution.py:903
  139.7 14.3 %conditional.5 = (bf16[4,64,768]{2,1,0:T(8,128)(2,1)}, bf16[4,64,768]{2,1,0:T(8,128)(2,1)}, bf16[120,768]{1,0:T(8,128)(2,1)S(1)}, bf16[120,768]{1,0:T(8,128)(2,1...) conditional(s32[]{:T(128)} %bitcast, () %tuple.32, ...), branch_computations={%region_4.5_spmd, %region_5.6_spmd} | conditional | bytes 14332268 | solution.py:1021
  146.2 4.4 %home_out.1 = (bf16[4,256,768]{2,1,0:T(8,128)(2,1)}, f32[8,128]{1,0:T(8,128)}) custom-call(s32[11]{0:T(128)S(1)} %get-tuple-element.71.refs_0_, bf16[4,256,768]{2,1,0:T(8,128)(2,1)S(1)} %get-tuple-element.72.refs_1_, bf16[4,64,768]{2,1,0:T(8,128)(2,1)} %get-tuple-element.73.refs_2_, bf16[4,64,768]{2,1,0:T(8,128)(2,1)} %get-tuple-element.74.refs_3_, ...), custom_call_target="tpu_custom_call" | custom-call | bytes 4722688 | tf_op jit(solution)/shard_map/cond/branch_1_fun/home_out/pallas_call | solution.py:157
  150.6 3.4 %collective-permute-done.17 = bf16[120,768]{1,0:T(8,128)(2,1)} collective-permute-done((bf16[120,768]{1,0:T(8,128)(2,1)}, bf16[120,768]{1,0:T(8,128)(2,1)}, u32[]{:S(2)}, u32[]{:S(2)}) %collective-permute-start.17) | collective-permute-done | bytes 184352 | tf_op jit(solution)/shard_map/cond/branch_1_fun/ppermute | solution.py:903
  161.5 5.8 %update_b.1 = (f32[838,1,768]{2,1,0:T(1,128)}, f32[838,1,768]{2,1,0:T(1,128)}, f32[838,1,768]{2,1,0:T(1,128)}, f32[8,128]{1,0:T(8,128)}) custom-call(s32[11]{0:T(128)S(1)} %concatenate.3.refs_0_, bf16[120,768]{1,0:T(8,128)(2,1)S(1)} %get-tuple-element.302.refs_1_, bf16[120,768]{1,0:T(8,128)(2,1)} %get-tuple-element.303.refs_2_, ...), custom_call_target="tpu_custom_call" | custom-call | bytes 16187392 | tf_op jit(solution)/shard_map/update_b/pallas_call | solution.py:157
  168.1 5.1 %home_grad.1 = (f32[4,256,768]{2,1,0:T(8,128)}, f32[8,128]{1,0:T(8,128)S(1)}) custom-call(s32[11]{0:T(128)S(1)} %concatenate.3.refs_0_, bf16[4,256,768]{2,1,0:T(8,128)(2,1)S(1)} %copy-done.20, bf16[4,256,768]{2,1,0:T(8,128)(2,1)S(1)} %copy-done, f32[8,768]{1,0:T(8,128)S(1)} %get-tuple-element.221.refs_3_.refs_11_.refs_7_.refs_10_.refs_14_, ...), custom_call_target="tpu_custom_call" | custom-call | bytes 7892992 | tf_op jit(solution)/shard_map/home_grad/pallas_call | solution.py:157
  174.2 8.2 %update_a.1 = (f32[384,768]{1,0:T(8,128)}, f32[384,768]{1,0:T(8,128)}, f32[384,768]{1,0:T(8,128)}, f32[838,1,768]{2,1,0:T(1,128)}, f32[838,1,768]{2,1,0:T(1,128)...) custom-call(s32[11]{0:T(128)S(1)} %concatenate.3.refs_0_, ...), custom_call_target="tpu_custom_call", output_to_operand_aliasing={{3}: (11, {}), {4}: (12, {}), {5}: (13, {})} | custom-call | bytes 31430656 | tf_op jit(solution)/shard_map/update_a/pallas_call | solution.py:157
  (176 shorter events, 90.9 us)
Async XLA Ops:
  8.2 9.8 %collective-permute-start.22 = (bf16[144,768]{1,0:T(8,128)(2,1)S(1)}, bf16[144,768]{1,0:T(8,128)(2,1)S(1)}, u32[]{:S(2)}, u32[]{:S(2)}) collective-permute-start(bf16[144,768]{1,0:T(8,128)(2,1)S(1)} %get-tuple-element.218), channel_id=1, source_target_pairs={{0,12},{4,8},{8,4},{12,0},{16,28},{20,24},{24,20},{28,16},{1,13},{... | collective-permute-start | bytes 663560 | tf_op jit(solution)/shard_map/ppermute | solution.py:903
  18.7 10.4 %collective-permute-start.23 = (bf16[4,128,768]{2,1,0:T(8,128)(2,1)S(1)}, bf16[4,128,768]{2,1,0:T(8,128)(2,1)S(1)}, u32[]{:S(2)}, u32[]{:S(2)}) collective-permute-start(bf16[4,128,768]{2,1,0:T(8,128)(2,1)S(1)} %get-tuple-element.220.refs_1_.refs_9_), channel_id=1, source_target_pairs={{0,1},{1,0},{2,3},{3,2},{4,5},{5,4},{6,7},{7,6},{8,9},{9,8},{10,11... | collective-permute-start | bytes 2359304 | tf_op jit(solution)/shard_map/ppermute | solution.py:903
  24.1 15.3 %collective-permute-start.28 = (bf16[128,768]{1,0:T(8,128)(2,1)S(1)}, bf16[128,768]{1,0:T(8,128)(2,1)S(1)}, u32[]{:S(2)}, u32[]{:S(2)}) collective-permute-start(bf16[128,768]{1,0:T(8,128)(2,1)S(1)} %get-tuple-element.235), channel_id=1, source_target_pairs={{0,4},{4,0},{8,12},{12,8},{16,20},{20,16},{24,28},{28,24},{1,5},{5... | collective-permute-start | bytes 589832 | tf_op jit(solution)/shard_map/ppermute | solution.py:903
  25.7 13.7 %collective-permute-start.29 = (bf16[128,768]{1,0:T(8,128)(2,1)S(1)}, bf16[128,768]{1,0:T(8,128)(2,1)S(1)}, u32[]{:S(2)}, u32[]{:S(2)}) collective-permute-start(bf16[128,768]{1,0:T(8,128)(2,1)S(1)} %get-tuple-element.236), channel_id=1, source_target_pairs={{0,8},{4,12},{8,0},{12,4},{16,24},{20,28},{24,16},{28,20},{1,9},{5... | collective-permute-start | bytes 589832 | tf_op jit(solution)/shard_map/ppermute | solution.py:903
  27.3 12.2 %collective-permute-start.30 = (bf16[128,768]{1,0:T(8,128)(2,1)S(1)}, bf16[128,768]{1,0:T(8,128)(2,1)S(1)}, u32[]{:S(2)}, u32[]{:S(2)}) collective-permute-start(bf16[128,768]{1,0:T(8,128)(2,1)S(1)} %get-tuple-element.237), channel_id=1, source_target_pairs={{0,12},{4,8},{8,4},{12,0},{16,28},{20,24},{24,20},{28,16},{1,13},{... | collective-permute-start | bytes 589832 | tf_op jit(solution)/shard_map/ppermute | solution.py:903
  62.8 18.7 %collective-permute-start.41 = (bf16[4,64,768]{2,1,0:T(8,128)(2,1)S(1)}, bf16[4,64,768]{2,1,0:T(8,128)(2,1)S(1)}, u32[]{:S(2)}, u32[]{:S(2)}) collective-permute-start(bf16[4,64,768]{2,1,0:T(8,128)(2,1)S(1)} %get-tuple-element.253.refs_9_), channel_id=1, source_target_pairs={{0,2},{1,3},{2,0},{3,1},{4,6},{5,7},{6,4},{7,5},{8,10},{9,11},{10,... | collective-permute-start | bytes 1179656 | tf_op jit(solution)/shard_map/ppermute | solution.py:903
  77.4 13.2 %collective-permute-start.43 = (bf16[192,768]{1,0:T(8,128)(2,1)S(1)}, bf16[192,768]{1,0:T(8,128)(2,1)S(1)}, u32[]{:S(2)}, u32[]{:S(2)}) collective-permute-start(bf16[192,768]{1,0:T(8,128)(2,1)S(1)} %get-tuple-element.279), channel_id=1, source_target_pairs={{0,4},{4,0},{8,12},{12,8},{16,20},{20,16},{24,28},{28,24},{1,5},{5... | collective-permute-start | bytes 884744 | tf_op jit(solution)/shard_map/ppermute | solution.py:903
  77.9 12.7 %collective-permute-start.44 = (bf16[192,768]{1,0:T(8,128)(2,1)S(1)}, bf16[192,768]{1,0:T(8,128)(2,1)S(1)}, u32[]{:S(2)}, u32[]{:S(2)}) collective-permute-start(bf16[192,768]{1,0:T(8,128)(2,1)S(1)} %get-tuple-element.280), channel_id=1, source_target_pairs={{0,8},{4,12},{8,0},{12,4},{16,24},{20,28},{24,16},{28,20},{1,9},{5... | collective-permute-start | bytes 884744 | tf_op jit(solution)/shard_map/ppermute | solution.py:903
  80.5 15.0 %collective-permute-start.45 = (bf16[192,768]{1,0:T(8,128)(2,1)S(1)}, bf16[192,768]{1,0:T(8,128)(2,1)S(1)}, u32[]{:S(2)}, u32[]{:S(2)}) collective-permute-start(bf16[192,768]{1,0:T(8,128)(2,1)S(1)} %get-tuple-element.281), channel_id=1, source_target_pairs={{0,12},{4,8},{8,4},{12,0},{16,28},{20,24},{24,20},{28,16},{1,13},{... | collective-permute-start | bytes 884744 | tf_op jit(solution)/shard_map/ppermute | solution.py:903
  101.0 16.8 %collective-permute-start.1 = (bf16[4,64,768]{2,1,0:T(8,128)(2,1)S(1)}, bf16[4,64,768]{2,1,0:T(8,128)(2,1)S(1)}, u32[]{:S(2)}, u32[]{:S(2)}) collective-permute-start(bf16[4,64,768]{2,1,0:T(8,128)(2,1)S(1)} %get-tuple-element.50), channel_id=1, source_target_pairs={{0,2},{1,3},{2,0},{3,1},{4,6},{5,7},{6,4},{7,5},{8,10},{9,11},{10,... | collective-permute-start | bytes 1179656 | tf_op jit(solution)/shard_map/cond/branch_1_fun/ppermute | solution.py:903
  102.2 23.2 %collective-permute-start.8 = (bf16[192,768]{1,0:T(8,128)(2,1)S(1)}, bf16[192,768]{1,0:T(8,128)(2,1)S(1)}, u32[]{:S(2)}, u32[]{:S(2)}) collective-permute-start(bf16[192,768]{1,0:T(8,128)(2,1)S(1)} %get-tuple-element.63.refs_0_), channel_id=1, source_target_pairs={{0,16},{4,20},{8,24},{12,28},{16,0},{20,4},{24,8},{28,12},{1,17},{... | collective-permute-start | bytes 884744 | tf_op jit(solution)/shard_map/cond/branch_1_fun/ppermute | solution.py:903
  105.4 9.8 %collective-permute-start.3 = (bf16[120,768]{1,0:T(8,128)(2,1)S(1)}, bf16[120,768]{1,0:T(8,128)(2,1)S(1)}, u32[]{:S(2)}, u32[]{:S(2)}) collective-permute-start(bf16[120,768]{1,0:T(8,128)(2,1)S(1)} %get-tuple-element.57), channel_id=1, source_target_pairs={{0,8},{4,12},{8,0},{12,4},{16,24},{20,28},{24,16},{28,20},{1,9},{5... | collective-permute-start | bytes 552968 | tf_op jit(solution)/shard_map/cond/branch_1_fun/ppermute | solution.py:903
  105.4 16.7 %collective-permute-start.4 = (bf16[120,768]{1,0:T(8,128)(2,1)S(1)}, bf16[120,768]{1,0:T(8,128)(2,1)S(1)}, u32[]{:S(2)}, u32[]{:S(2)}) collective-permute-start(bf16[120,768]{1,0:T(8,128)(2,1)S(1)} %get-tuple-element.58), channel_id=1, source_target_pairs={{0,12},{4,8},{8,4},{12,0},{16,28},{20,24},{24,20},{28,16},{1,13},{... | collective-permute-start | bytes 552968 | tf_op jit(solution)/shard_map/cond/branch_1_fun/ppermute | solution.py:903
  110.6 12.4 %collective-permute-start.5 = (bf16[64,768]{1,0:T(8,128)(2,1)S(1)}, bf16[64,768]{1,0:T(8,128)(2,1)S(1)}, u32[]{:S(2)}, u32[]{:S(2)}) collective-permute-start(bf16[64,768]{1,0:T(8,128)(2,1)S(1)} %get-tuple-element.60), channel_id=1, source_target_pairs={{0,4},{4,0},{8,12},{12,8},{16,20},{20,16},{24,28},{28,24},{1,5},{5... | collective-permute-start | bytes 294920 | tf_op jit(solution)/shard_map/cond/branch_1_fun/ppermute | solution.py:903
  125.5 14.2 %collective-permute-start.46 = (bf16[4,64,768]{2,1,0:T(8,128)(2,1)}, bf16[4,64,768]{2,1,0:T(8,128)(2,1)}, u32[]{:S(2)}, u32[]{:S(2)}) collective-permute-start(bf16[4,64,768]{2,1,0:T(8,128)(2,1)} %get-tuple-element.298), channel_id=1, source_target_pairs={{0,2},{1,3},{2,0},{3,1},{4,6},{5,7},{6,4},{7,5},{8,10},{9,11},{10,... | collective-permute-start | bytes 1179656 | tf_op jit(solution)/shard_map/ppermute | solution.py:903
  126.4 12.3 %collective-permute-start.12 = (bf16[120,768]{1,0:T(8,128)(2,1)}, bf16[120,768]{1,0:T(8,128)(2,1)S(1)}, u32[]{:S(2)}, u32[]{:S(2)}) collective-permute-start(bf16[120,768]{1,0:T(8,128)(2,1)} %get-tuple-element.68.refs_0_), channel_id=1, source_target_pairs={{0,16},{4,20},{8,24},{12,28},{16,0},{20,4},{24,8},{28,12},{1,17},{... | collective-permute-start | bytes 552968 | tf_op jit(solution)/shard_map/cond/branch_1_fun/ppermute | solution.py:903
  140.4 13.6 %collective-permute-start.13 = (bf16[4,64,768]{2,1,0:T(8,128)(2,1)}, bf16[4,64,768]{2,1,0:T(8,128)(2,1)}, u32[]{:S(2)}, u32[]{:S(2)}) collective-permute-start(bf16[4,64,768]{2,1,0:T(8,128)(2,1)} %get-tuple-element.69), channel_id=1, source_target_pairs={{0,2},{1,3},{2,0},{3,1},{4,6},{5,7},{6,4},{7,5},{8,10},{9,11},{10,... | collective-permute-start | bytes 1179656 | tf_op jit(solution)/shard_map/cond/branch_1_fun/ppermute | solution.py:903
  141.5 12.5 %collective-permute-start.14 = (bf16[4,64,768]{2,1,0:T(8,128)(2,1)}, bf16[4,64,768]{2,1,0:T(8,128)(2,1)}, u32[]{:S(2)}, u32[]{:S(2)}) collective-permute-start(bf16[4,64,768]{2,1,0:T(8,128)(2,1)} %get-tuple-element.69), channel_id=1, source_target_pairs={{0,1},{1,0},{2,3},{3,2},{4,5},{5,4},{6,7},{7,6},{8,9},{9,8},{10,11... | collective-permute-start | bytes 1179656 | tf_op jit(solution)/shard_map/cond/branch_1_fun/ppermute | solution.py:903
  143.1 11.0 %collective-permute-start.17 = (bf16[120,768]{1,0:T(8,128)(2,1)}, bf16[120,768]{1,0:T(8,128)(2,1)}, u32[]{:S(2)}, u32[]{:S(2)}) collective-permute-start(bf16[120,768]{1,0:T(8,128)(2,1)} %copy-done.23), channel_id=1, source_target_pairs={{0,12},{4,8},{8,4},{12,0},{16,28},{20,24},{24,20},{28,16},{1,13},{... | collective-permute-start | bytes 552968 | tf_op jit(solution)/shard_map/cond/branch_1_fun/ppermute | solution.py:903
  154.1 13.3 %collective-permute-start.47 = (bf16[4,64,768]{2,1,0:T(8,128)(2,1)}, bf16[4,64,768]{2,1,0:T(8,128)(2,1)S(1)}, u32[]{:S(2)}, u32[]{:S(2)}) collective-permute-start(bf16[4,64,768]{2,1,0:T(8,128)(2,1)} %get-tuple-element.300.refs_5_), channel_id=1, source_target_pairs={{0,1},{1,0},{2,3},{3,2},{4,5},{5,4},{6,7},{7,6},{8,9},{9,8},{10,11... | collective-permute-start | bytes 1179656 | tf_op jit(solution)/shard_map/ppermute | solution.py:903
  154.1 19.1 %collective-permute-start.50 = (bf16[192,768]{1,0:T(8,128)(2,1)}, bf16[192,768]{1,0:T(8,128)(2,1)S(1)}, u32[]{:S(2)}, u32[]{:S(2)}) collective-permute-start(bf16[192,768]{1,0:T(8,128)(2,1)} %copy-done.21), channel_id=1, source_target_pairs={{0,4},{4,0},{8,12},{12,8},{16,20},{20,16},{24,28},{28,24},{1,5},{5... | collective-permute-start | bytes 884744 | tf_op jit(solution)/shard_map/ppermute | solution.py:903
  154.7 18.5 %collective-permute-start.51 = (bf16[192,768]{1,0:T(8,128)(2,1)}, bf16[192,768]{1,0:T(8,128)(2,1)S(1)}, u32[]{:S(2)}, u32[]{:S(2)}) collective-permute-start(bf16[192,768]{1,0:T(8,128)(2,1)} %copy-done.21), channel_id=1, source_target_pairs={{0,8},{4,12},{8,0},{12,4},{16,24},{20,28},{24,16},{28,20},{1,9},{5... | collective-permute-start | bytes 884744 | tf_op jit(solution)/shard_map/ppermute | solution.py:903
  155.4 17.8 %collective-permute-start.52 = (bf16[192,768]{1,0:T(8,128)(2,1)}, bf16[192,768]{1,0:T(8,128)(2,1)S(1)}, u32[]{:S(2)}, u32[]{:S(2)}) collective-permute-start(bf16[192,768]{1,0:T(8,128)(2,1)} %copy-done.21), channel_id=1, source_target_pairs={{0,12},{4,8},{8,4},{12,0},{16,28},{20,24},{24,20},{28,16},{1,13},{... | collective-permute-start | bytes 884744 | tf_op jit(solution)/shard_map/ppermute | solution.py:903
  160.5 21.9 %collective-permute-start.49 = (f32[8,768]{1,0:T(8,128)S(1)}, f32[8,768]{1,0:T(8,128)S(1)}, u32[]{:S(2)}, u32[]{:S(2)}) collective-permute-start(f32[8,768]{1,0:T(8,128)S(1)} %add_small.1.refs_8_.refs_1_), channel_id=1, source_target_pairs={{0,2},{1,3},{2,0},{3,1},{4,6},{5,7},{6,4},{7,5},{8,10},{9,11},{10,... | collective-permute-start | bytes 73736 | tf_op jit(solution)/shard_map/ppermute | solution.py:903
  (57 other events, 327.2 us)

commit v2 on v1

--- a/solution.py
+++ b/solution.py
@@ -150,7 +150,7 @@
     spec = pltpu.PrefetchScalarGridSpec(
         num_scalar_prefetch=0 if prefetch is None else 1,
         grid=grid,
-        in_specs=list(in_specs) + [pl.BlockSpec(memory_space=pl.ANY)] * len(after),
+        in_specs=list(in_specs) + [token_spec(a) for a in after],
         out_specs=out_specs,
         scratch_shapes=scratch,
     )
@@ -165,6 +165,10 @@
         input_output_aliases=aliases or {},
         name=name,
     )(*(() if prefetch is None else (prefetch,)), *ins, *after)
+
+
+def token_spec(array):
+    return whole((8, LANES)) if array.shape == (8, LANES) else pl.BlockSpec(memory_space=pl.ANY)
 
 
 STEP = []
@@ -1193,21 +1197,22 @@
     grad_parts = (own_grad, x_grad, core_grad, trade("head", 1)(x_grad))
 
     quarter = whole((SEG2, D))
-    small, norm = call(
+    small, norm, done_small = call(
         small_kernel, "small", (1,), sums2, [quarter] * 4, [sds((SMALL, D)), sds((8, D))],
-        [whole((SMALL, D)), whole((8, D))], prefetch=at,
-    )
-    eight = whole((8, D))
-    norm = call(
-        add_small_kernel, "add_small", (1,), (norm, trade("head", 1)(norm)), [eight] * 2, [sds((8, D))], [eight]
-    )[0]
-    norms = [norm, trade("head", 2)(norm)]
+        [whole((SMALL, D)), whole((8, D))], prefetch=at, token=True,
+    )
     *in_half, done_b = call(
         functools.partial(update_b_kernel, rate=RATES[1] / root), "update_b", (1,),
         (*sums2, *turned3), [quarter] * 4 + [hbm] * 3, turned_shape, [hbm] * 3,
         scratch=[pltpu.VMEM((GRP * SEG2, D), F32)] + buffers, prefetch=at,
-        after=(norm,), vmem=56, token=True,
-    )
+        after=(done_small,), vmem=56, token=True,
+    )
+    eight = whole((8, D))
+    norm = call(
+        add_small_kernel, "add_small", (1,), (norm, trade("head", 1)(norm)), [eight] * 2, [sds((8, D))], [eight],
+        after=(done_b,),
+    )[0]
+    norms = [norm, trade("head", 2)(norm)]
     input_grad, done_grad = home(
         home_grad_kernel, "home_grad", at, (block_in, cotangent, vecs), (None, None, (8, D)),
         grad_parts, F32, (done_b,),

time: 185 us -> 184 us (level)
  transfers between devices with their start and end apart: 53 -> 53, of which waited for: 20 -> 19; matrix products, arithmetic and copies ran while one was open for 1% -> 1% of each run, Pallas kernels for 37% -> 37%
where the time goes in v2:
time: 184 us; the launch traced here: 183 us
  Pallas kernels  81.6 us (44%)
  starting transfers between devices  54.6 us (30%)
  waiting for transfers between devices  40.5 us (22%)
  local copies, waits for them, and re-layouts  5.12 us (3%)
    pallas_call x33, Pallas kernels, call(): pl.pallas_call(body, grid_spec=spec, out_shape=outs, compiler_params=pltp...  81.6 us
    ppermute x53, starting transfers between devices, trade(): return lambda array: lax.ppermute(array, axis, pairs)  54.6 us
    ppermute x53, waiting for transfers between devices, trade(): return lambda array: lax.ppermute(array, axis, pairs)  40.5 us
  transfers between devices with their start and end apart: 53, of which 19 were waited for; matrix products, arithmetic and copies ran while one was open for 1% of the time, Pallas kernels for 37%

profile of v2, /device:TPU:0, one launch (start us, length us, event | category | flops | bytes accessed | tf_op | source)
XLA Modules:
  0.0 183.5 jit_solution(1608597767346768592)
XLA Ops:
  3.6 3.0 %collective-permute-start.20 = (bf16[144,768]{1,0:T(8,128)(2,1)S(1)}, bf16[144,768]{1,0:T(8,128)(2,1)S(1)}, u32[]{:S(2)}, u32[]{:S(2)}) collective-permute-start(bf16[144,768]{1,0:T(8,128)(2,1)S(1)} %get-tuple-element.217), channel_id=1, source_target_pairs={{0,4},{4,0},{8,12},{12,8},{16,20},{20,16},{24,28},{28,24},{1,5},{5... | collective-permute-start | bytes 663560 | tf_op jit(solution)/shard_map/ppermute | solution.py:907
  12.1 2.9 %collective-permute-done.21.refs_3_ = bf16[144,768]{1,0:T(8,128)(2,1)S(1)} collective-permute-done((bf16[144,768]{1,0:T(8,128)(2,1)S(1)}, bf16[144,768]{1,0:T(8,128)(2,1)S(1)}, u32[]{:S(2)}, u32[]{:S(2)}) %collective-permute-start.21) | collective-permute-done | bytes 221216 | tf_op jit(solution)/shard_map/ppermute | solution.py:907
  15.0 3.1 %collective-permute-done.22.refs_4_ = bf16[144,768]{1,0:T(8,128)(2,1)S(1)} collective-permute-done((bf16[144,768]{1,0:T(8,128)(2,1)S(1)}, bf16[144,768]{1,0:T(8,128)(2,1)S(1)}, u32[]{:S(2)}, u32[]{:S(2)}) %collective-permute-start.22) | collective-permute-done | bytes 221216 | tf_op jit(solution)/shard_map/ppermute | solution.py:907
  29.1 4.6 %first.1 = (bf16[1024,768]{1,0:T(8,128)(2,1)S(1)}, f32[1024,384]{1,0:T(8,128)S(1)}, f32[1024,128]{1,0:T(8,128)S(1)}, f32[8,1024]{1,0:T(8,128)S(1)}, f32[8,128]{1,0:T(8,128)}) custom-call(s32[11]{0:T(128)S(1)} %concatenate.3.refs_0_, bf16[4,128,768]{2,1,0:T(8,128)(2,1)S(1)} %get-tuple-element.221.refs_1_.refs_9_, ...), custom_call_target="tpu_custom_call" | custom-call | flops 805306368 | bytes 6782976 | tf_op jit(solution)/shard_map/first/pallas_call | solution.py:157
  33.7 5.8 %mix.1 = (f32[1024,384]{1,0:T(8,128)S(1)}, f32[1024,384]{1,0:T(8,128)S(1)}, f32[1024,384]{1,0:T(8,128)S(1)}, bf16[1024,384]{1,0:T(8,128)(2,1)S(1)}, f32[1024,64]...) custom-call(s32[11]{0:T(128)S(1)} %concatenate.3.refs_0_, ...), custom_call_target="tpu_custom_call" | custom-call | flops 1107296256 | bytes 12641024 | tf_op jit(solution)/shard_map/mix/pallas_call | solution.py:157
  40.5 2.9 %collective-permute-start.32 = (bf16[384,128]{1,0:T(8,128)(2,1)S(1)}, bf16[384,128]{1,0:T(8,128)(2,1)S(1)}, u32[]{:S(2)}, u32[]{:S(2)}) collective-permute-start(bf16[384,128]{1,0:T(8,128)(2,1)S(1)} %get-tuple-element.239.refs_5_), channel_id=1, source_target_pairs={{0,16},{4,20},{8,24},{12,28},{16,0},{20,4},{24,8},{28,12},{1,17},{... | collective-permute-start | bytes 294920 | tf_op jit(solution)/shard_map/ppermute | solution.py:907
  43.4 3.3 %local.1 = (f32[1024,384]{1,0:T(8,128)S(1)}, f32[1024,384]{1,0:T(8,128)S(1)}, bf16[1024,768]{1,0:T(8,128)(2,1)S(1)}) custom-call(s32[11]{0:T(128)S(1)} %concatenate.3.refs_0_, bf16[1024,384]{1,0:T(8,128)(2,1)S(1)} %get-tuple-element.229.refs_1_, f32[1024,384]{1,0:T(8,128)S(1)} %get-tuple-element.230.refs_2_.refs_7_, ...), custom_call_target="tpu_custom_call" | custom-call | flops 1409286144 | bytes 11132928 | tf_op jit(solution)/shard_map/local/pallas_call | solution.py:157
  56.2 3.4 %ungate.1 = (f32[1024,384]{1,0:T(8,128)S(1)}, bf16[1024,384]{1,0:T(8,128)(2,1)S(1)}, bf16[1024,384]{1,0:T(8,128)(2,1)S(1)}, bf16[384,128]{1,0:T(8,128)(2,1)S(1)}...) custom-call(s32[11]{0:T(128)S(1)} %concatenate.3.refs_0_, ...), custom_call_target="tpu_custom_call" | custom-call | flops 704643072 | bytes 11079680 | tf_op jit(solution)/shard_map/ungate/pallas_call | solution.py:157
  64.4 6.8 %inner.1 = (f32[1024,384]{1,0:T(8,128)S(1)}, f32[1024,128]{1,0:T(8,128)S(1)}, f32[1024,128]{1,0:T(8,128)S(1)}, f32[1024,128]{1,0:T(8,128)S(1)}, f32[4,384,128]{2,1,0:T(8,128)S(1)}) custom-call(s32[11]{0:T(128)S(1)} %concatenate.3.refs_0_, bf16[1024,384]{1,0:T(8,128)(2,1)S(1)} %get-tuple-element.229.refs_1_, ...), custom_call_target="tpu_custom_call" | custom-call | bytes 8257536 | tf_op jit(solution)/shard_map/inner/pallas_call | solution.py:157
  71.5 5.8 %back.1 = (f32[1024,384]{1,0:T(8,128)S(1)}, f32[8,384]{1,0:T(8,128)S(1)}, bf16[512,128]{1,0:T(8,128)(2,1)S(1)}, bf16[512,128]{1,0:T(8,128)(2,1)S(1)}, bf16[512,1...) custom-call(s32[11]{0:T(128)S(1)} %concatenate.3.refs_0_, ...), custom_call_target="tpu_custom_call" | custom-call | flops 402653184 | bytes 12201984 | tf_op jit(solution)/shard_map/back/pallas_call | solution.py:157
  82.9 5.3 %last_x.1 = (f32[1024,768]{1,0:T(8,128)S(1)}, f32[16,384]{1,0:T(8,128)S(1)}, f32[480,768]{1,0:T(8,128)S(1)}) custom-call(s32[11]{0:T(128)S(1)} %concatenate.3.refs_0_, f32[1024,384]{1,0:T(8,128)S(1)} %get-tuple-element.267.refs_1_.refs_2_, f32[1024,384]{1,0:T(8,128)S(1)} %get-tuple-element.267.refs_1_.refs_2_, ...), custom_call_target="tpu_custom_call" | custom-call | flops 2415919104 | bytes 13468416 | tf_op jit(solution)/shard_map/last_x/pallas_call | solution.py:157
  90.6 4.9 %collective-permute-done.45.refs_3_ = bf16[192,768]{1,0:T(8,128)(2,1)S(1)} collective-permute-done((bf16[192,768]{1,0:T(8,128)(2,1)S(1)}, bf16[192,768]{1,0:T(8,128)(2,1)S(1)}, u32[]{:S(2)}, u32[]{:S(2)}) %collective-permute-start.45) | collective-permute-done | bytes 294944 | tf_op jit(solution)/shard_map/ppermute | solution.py:907
  97.8 27.7 %conditional.3 = (bf16[64,768]{1,0:T(8,128)(2,1)}, bf16[64,768]{1,0:T(8,128)(2,1)S(1)}, bf16[64,768]{1,0:T(8,128)(2,1)S(1)}, bf16[64,768]{1,0:T(8,128)(2,1)}, bf...) conditional(s32[]{:T(128)} %bitcast, () %tuple.34, ...), branch_computations={%region_0.1_spmd, %region_1.2_spmd} | conditional | bytes 16208288 | solution.py:1025
  107.4 3.2 %collective-permute-done.2.refs_1_ = bf16[120,768]{1,0:T(8,128)(2,1)S(1)} collective-permute-done((bf16[120,768]{1,0:T(8,128)(2,1)S(1)}, bf16[120,768]{1,0:T(8,128)(2,1)S(1)}, u32[]{:S(2)}, u32[]{:S(2)}) %collective-permute-start.2) | collective-permute-done | bytes 184352 | tf_op jit(solution)/shard_map/cond/branch_1_fun/ppermute | solution.py:907
  112.1 3.2 %collective-permute-done.3.refs_2_ = bf16[120,768]{1,0:T(8,128)(2,1)S(1)} collective-permute-done((bf16[120,768]{1,0:T(8,128)(2,1)S(1)}, bf16[120,768]{1,0:T(8,128)(2,1)S(1)}, u32[]{:S(2)}, u32[]{:S(2)}) %collective-permute-start.3) | collective-permute-done | bytes 184352 | tf_op jit(solution)/shard_map/cond/branch_1_fun/ppermute | solution.py:907
  126.4 13.3 %conditional.4 = (bf16[4,64,768]{2,1,0:T(8,128)(2,1)}, bf16[120,768]{1,0:T(8,128)(2,1)S(1)}) conditional(s32[]{:T(128)} %bitcast, () %tuple.33, (bf16[64,768]{1,0:T(8,128)(2,1)S(1)}, bf16[64,768]{1,0:T(8,128)(2,1)S(1)}, bf16[64,768]{1,0:T(8,128)(2,1)}, bf16[64,768]{1,0:T(8,128)(2,1)}, bf16[120,768]{1,0:T(8,128)(2,1)}) %tuple.36), branch_computations={%region_2.3_spmd, %region_3.4_spmd} | conditional | bytes 3256496 | solution.py:1025
  130.8 3.3 %collective-permute-done.10.refs_2_ = bf16[64,768]{1,0:T(8,128)(2,1)S(1)} collective-permute-done((bf16[64,768]{1,0:T(8,128)(2,1)S(1)}, bf16[64,768]{1,0:T(8,128)(2,1)S(1)}, u32[]{:S(2)}, u32[]{:S(2)}) %collective-permute-start.10) | collective-permute-done | bytes 98336 | tf_op jit(solution)/shard_map/cond/branch_1_fun/ppermute | solution.py:907
  134.1 2.9 %collective-permute-done.11.refs_3_ = bf16[64,768]{1,0:T(8,128)(2,1)S(1)} collective-permute-done((bf16[64,768]{1,0:T(8,128)(2,1)}, bf16[64,768]{1,0:T(8,128)(2,1)S(1)}, u32[]{:S(2)}, u32[]{:S(2)}) %collective-permute-start.11) | collective-permute-done | bytes 98336 | tf_op jit(solution)/shard_map/cond/branch_1_fun/ppermute | solution.py:907
  139.7 14.3 %conditional.5 = (bf16[4,64,768]{2,1,0:T(8,128)(2,1)}, bf16[4,64,768]{2,1,0:T(8,128)(2,1)}, bf16[120,768]{1,0:T(8,128)(2,1)S(1)}, bf16[120,768]{1,0:T(8,128)(2,1...) conditional(s32[]{:T(128)} %bitcast, () %tuple.32, ...), branch_computations={%region_4.5_spmd, %region_5.6_spmd} | conditional | bytes 14332268 | solution.py:1025
  146.2 4.4 %home_out.1 = (bf16[4,256,768]{2,1,0:T(8,128)(2,1)}, f32[8,128]{1,0:T(8,128)}) custom-call(s32[11]{0:T(128)S(1)} %get-tuple-element.71.refs_0_, bf16[4,256,768]{2,1,0:T(8,128)(2,1)S(1)} %get-tuple-element.72.refs_1_, bf16[4,64,768]{2,1,0:T(8,128)(2,1)} %get-tuple-element.73.refs_2_, bf16[4,64,768]{2,1,0:T(8,128)(2,1)} %get-tuple-element.74.refs_3_, ...), custom_call_target="tpu_custom_call" | custom-call | bytes 4722688 | tf_op jit(solution)/shard_map/cond/branch_1_fun/home_out/pallas_call | solution.py:157
  150.6 3.4 %collective-permute-done.17 = bf16[120,768]{1,0:T(8,128)(2,1)} collective-permute-done((bf16[120,768]{1,0:T(8,128)(2,1)}, bf16[120,768]{1,0:T(8,128)(2,1)}, u32[]{:S(2)}, u32[]{:S(2)}) %collective-permute-start.17) | collective-permute-done | bytes 184352 | tf_op jit(solution)/shard_map/cond/branch_1_fun/ppermute | solution.py:907
  160.1 5.8 %update_b.1 = (f32[838,1,768]{2,1,0:T(1,128)}, f32[838,1,768]{2,1,0:T(1,128)}, f32[838,1,768]{2,1,0:T(1,128)}, f32[8,128]{1,0:T(8,128)}) custom-call(s32[11]{0:T(128)S(1)} %concatenate.3.refs_0_, bf16[120,768]{1,0:T(8,128)(2,1)S(1)} %get-tuple-element.303.refs_1_, bf16[120,768]{1,0:T(8,128)(2,1)} %get-tuple-element.304.refs_2_, ...), custom_call_target="tpu_custom_call" | custom-call | bytes 16187392 | tf_op jit(solution)/shard_map/update_b/pallas_call | solution.py:157
  167.5 5.1 %home_grad.1 = (f32[4,256,768]{2,1,0:T(8,128)}, f32[8,128]{1,0:T(8,128)S(1)}) custom-call(s32[11]{0:T(128)S(1)} %concatenate.3.refs_0_, bf16[4,256,768]{2,1,0:T(8,128)(2,1)S(1)} %copy-done.19, bf16[4,256,768]{2,1,0:T(8,128)(2,1)S(1)} %copy-done, f32[8,768]{1,0:T(8,128)S(1)} %get-tuple-element.222.refs_3_.refs_11_.refs_7_.refs_10_.refs_14_, ...), custom_call_target="tpu_custom_call" | custom-call | bytes 7892992 | tf_op jit(solution)/shard_map/home_grad/pallas_call | solution.py:157
  173.7 8.2 %update_a.1 = (f32[384,768]{1,0:T(8,128)}, f32[384,768]{1,0:T(8,128)}, f32[384,768]{1,0:T(8,128)}, f32[838,1,768]{2,1,0:T(1,128)}, f32[838,1,768]{2,1,0:T(1,128)...) custom-call(s32[11]{0:T(128)S(1)} %concatenate.3.refs_0_, ...), custom_call_target="tpu_custom_call", output_to_operand_aliasing={{3}: (11, {}), {4}: (12, {}), {5}: (13, {})} | custom-call | bytes 31430656 | tf_op jit(solution)/shard_map/update_a/pallas_call | solution.py:157
  (174 shorter events, 90.4 us)
Async XLA Ops:
  8.2 9.8 %collective-permute-start.22 = (bf16[144,768]{1,0:T(8,128)(2,1)S(1)}, bf16[144,768]{1,0:T(8,128)(2,1)S(1)}, u32[]{:S(2)}, u32[]{:S(2)}) collective-permute-start(bf16[144,768]{1,0:T(8,128)(2,1)S(1)} %get-tuple-element.219), channel_id=1, source_target_pairs={{0,12},{4,8},{8,4},{12,0},{16,28},{20,24},{24,20},{28,16},{1,13},{... | collective-permute-start | bytes 663560 | tf_op jit(solution)/shard_map/ppermute | solution.py:907
  18.7 10.4 %collective-permute-start.23 = (bf16[4,128,768]{2,1,0:T(8,128)(2,1)S(1)}, bf16[4,128,768]{2,1,0:T(8,128)(2,1)S(1)}, u32[]{:S(2)}, u32[]{:S(2)}) collective-permute-start(bf16[4,128,768]{2,1,0:T(8,128)(2,1)S(1)} %get-tuple-element.221.refs_1_.refs_9_), channel_id=1, source_target_pairs={{0,1},{1,0},{2,3},{3,2},{4,5},{5,4},{6,7},{7,6},{8,9},{9,8},{10,11... | collective-permute-start | bytes 2359304 | tf_op jit(solution)/shard_map/ppermute | solution.py:907
  24.1 15.3 %collective-permute-start.28 = (bf16[128,768]{1,0:T(8,128)(2,1)S(1)}, bf16[128,768]{1,0:T(8,128)(2,1)S(1)}, u32[]{:S(2)}, u32[]{:S(2)}) collective-permute-start(bf16[128,768]{1,0:T(8,128)(2,1)S(1)} %get-tuple-element.236), channel_id=1, source_target_pairs={{0,4},{4,0},{8,12},{12,8},{16,20},{20,16},{24,28},{28,24},{1,5},{5... | collective-permute-start | bytes 589832 | tf_op jit(solution)/shard_map/ppermute | solution.py:907
  25.7 13.7 %collective-permute-start.29 = (bf16[128,768]{1,0:T(8,128)(2,1)S(1)}, bf16[128,768]{1,0:T(8,128)(2,1)S(1)}, u32[]{:S(2)}, u32[]{:S(2)}) collective-permute-start(bf16[128,768]{1,0:T(8,128)(2,1)S(1)} %get-tuple-element.237), channel_id=1, source_target_pairs={{0,8},{4,12},{8,0},{12,4},{16,24},{20,28},{24,16},{28,20},{1,9},{5... | collective-permute-start | bytes 589832 | tf_op jit(solution)/shard_map/ppermute | solution.py:907
  27.3 12.2 %collective-permute-start.30 = (bf16[128,768]{1,0:T(8,128)(2,1)S(1)}, bf16[128,768]{1,0:T(8,128)(2,1)S(1)}, u32[]{:S(2)}, u32[]{:S(2)}) collective-permute-start(bf16[128,768]{1,0:T(8,128)(2,1)S(1)} %get-tuple-element.238), channel_id=1, source_target_pairs={{0,12},{4,8},{8,4},{12,0},{16,28},{20,24},{24,20},{28,16},{1,13},{... | collective-permute-start | bytes 589832 | tf_op jit(solution)/shard_map/ppermute | solution.py:907
  62.8 18.7 %collective-permute-start.41 = (bf16[4,64,768]{2,1,0:T(8,128)(2,1)S(1)}, bf16[4,64,768]{2,1,0:T(8,128)(2,1)S(1)}, u32[]{:S(2)}, u32[]{:S(2)}) collective-permute-start(bf16[4,64,768]{2,1,0:T(8,128)(2,1)S(1)} %get-tuple-element.254.refs_9_), channel_id=1, source_target_pairs={{0,2},{1,3},{2,0},{3,1},{4,6},{5,7},{6,4},{7,5},{8,10},{9,11},{10,... | collective-permute-start | bytes 1179656 | tf_op jit(solution)/shard_map/ppermute | solution.py:907
  77.4 13.2 %collective-permute-start.43 = (bf16[192,768]{1,0:T(8,128)(2,1)S(1)}, bf16[192,768]{1,0:T(8,128)(2,1)S(1)}, u32[]{:S(2)}, u32[]{:S(2)}) collective-permute-start(bf16[192,768]{1,0:T(8,128)(2,1)S(1)} %get-tuple-element.280), channel_id=1, source_target_pairs={{0,4},{4,0},{8,12},{12,8},{16,20},{20,16},{24,28},{28,24},{1,5},{5... | collective-permute-start | bytes 884744 | tf_op jit(solution)/shard_map/ppermute | solution.py:907
  77.9 12.7 %collective-permute-start.44 = (bf16[192,768]{1,0:T(8,128)(2,1)S(1)}, bf16[192,768]{1,0:T(8,128)(2,1)S(1)}, u32[]{:S(2)}, u32[]{:S(2)}) collective-permute-start(bf16[192,768]{1,0:T(8,128)(2,1)S(1)} %get-tuple-element.281), channel_id=1, source_target_pairs={{0,8},{4,12},{8,0},{12,4},{16,24},{20,28},{24,16},{28,20},{1,9},{5... | collective-permute-start | bytes 884744 | tf_op jit(solution)/shard_map/ppermute | solution.py:907
  80.5 15.0 %collective-permute-start.45 = (bf16[192,768]{1,0:T(8,128)(2,1)S(1)}, bf16[192,768]{1,0:T(8,128)(2,1)S(1)}, u32[]{:S(2)}, u32[]{:S(2)}) collective-permute-start(bf16[192,768]{1,0:T(8,128)(2,1)S(1)} %get-tuple-element.282), channel_id=1, source_target_pairs={{0,12},{4,8},{8,4},{12,0},{16,28},{20,24},{24,20},{28,16},{1,13},{... | collective-permute-start | bytes 884744 | tf_op jit(solution)/shard_map/ppermute | solution.py:907
  101.0 16.8 %collective-permute-start.1 = (bf16[4,64,768]{2,1,0:T(8,128)(2,1)S(1)}, bf16[4,64,768]{2,1,0:T(8,128)(2,1)S(1)}, u32[]{:S(2)}, u32[]{:S(2)}) collective-permute-start(bf16[4,64,768]{2,1,0:T(8,128)(2,1)S(1)} %get-tuple-element.50), channel_id=1, source_target_pairs={{0,2},{1,3},{2,0},{3,1},{4,6},{5,7},{6,4},{7,5},{8,10},{9,11},{10,... | collective-permute-start | bytes 1179656 | tf_op jit(solution)/shard_map/cond/branch_1_fun/ppermute | solution.py:907
  102.2 23.2 %collective-permute-start.8 = (bf16[192,768]{1,0:T(8,128)(2,1)S(1)}, bf16[192,768]{1,0:T(8,128)(2,1)S(1)}, u32[]{:S(2)}, u32[]{:S(2)}) collective-permute-start(bf16[192,768]{1,0:T(8,128)(2,1)S(1)} %get-tuple-element.63.refs_0_), channel_id=1, source_target_pairs={{0,16},{4,20},{8,24},{12,28},{16,0},{20,4},{24,8},{28,12},{1,17},{... | collective-permute-start | bytes 884744 | tf_op jit(solution)/shard_map/cond/branch_1_fun/ppermute | solution.py:907
  105.4 9.8 %collective-permute-start.3 = (bf16[120,768]{1,0:T(8,128)(2,1)S(1)}, bf16[120,768]{1,0:T(8,128)(2,1)S(1)}, u32[]{:S(2)}, u32[]{:S(2)}) collective-permute-start(bf16[120,768]{1,0:T(8,128)(2,1)S(1)} %get-tuple-element.57), channel_id=1, source_target_pairs={{0,8},{4,12},{8,0},{12,4},{16,24},{20,28},{24,16},{28,20},{1,9},{5... | collective-permute-start | bytes 552968 | tf_op jit(solution)/shard_map/cond/branch_1_fun/ppermute | solution.py:907
  105.4 16.7 %collective-permute-start.4 = (bf16[120,768]{1,0:T(8,128)(2,1)S(1)}, bf16[120,768]{1,0:T(8,128)(2,1)S(1)}, u32[]{:S(2)}, u32[]{:S(2)}) collective-permute-start(bf16[120,768]{1,0:T(8,128)(2,1)S(1)} %get-tuple-element.58), channel_id=1, source_target_pairs={{0,12},{4,8},{8,4},{12,0},{16,28},{20,24},{24,20},{28,16},{1,13},{... | collective-permute-start | bytes 552968 | tf_op jit(solution)/shard_map/cond/branch_1_fun/ppermute | solution.py:907
  110.6 12.4 %collective-permute-start.5 = (bf16[64,768]{1,0:T(8,128)(2,1)S(1)}, bf16[64,768]{1,0:T(8,128)(2,1)S(1)}, u32[]{:S(2)}, u32[]{:S(2)}) collective-permute-start(bf16[64,768]{1,0:T(8,128)(2,1)S(1)} %get-tuple-element.60), channel_id=1, source_target_pairs={{0,4},{4,0},{8,12},{12,8},{16,20},{20,16},{24,28},{28,24},{1,5},{5... | collective-permute-start | bytes 294920 | tf_op jit(solution)/shard_map/cond/branch_1_fun/ppermute | solution.py:907
  125.5 14.2 %collective-permute-start.46 = (bf16[4,64,768]{2,1,0:T(8,128)(2,1)}, bf16[4,64,768]{2,1,0:T(8,128)(2,1)}, u32[]{:S(2)}, u32[]{:S(2)}) collective-permute-start(bf16[4,64,768]{2,1,0:T(8,128)(2,1)} %get-tuple-element.299), channel_id=1, source_target_pairs={{0,2},{1,3},{2,0},{3,1},{4,6},{5,7},{6,4},{7,5},{8,10},{9,11},{10,... | collective-permute-start | bytes 1179656 | tf_op jit(solution)/shard_map/ppermute | solution.py:907
  126.4 12.3 %collective-permute-start.12 = (bf16[120,768]{1,0:T(8,128)(2,1)}, bf16[120,768]{1,0:T(8,128)(2,1)S(1)}, u32[]{:S(2)}, u32[]{:S(2)}) collective-permute-start(bf16[120,768]{1,0:T(8,128)(2,1)} %get-tuple-element.68.refs_0_), channel_id=1, source_target_pairs={{0,16},{4,20},{8,24},{12,28},{16,0},{20,4},{24,8},{28,12},{1,17},{... | collective-permute-start | bytes 552968 | tf_op jit(solution)/shard_map/cond/branch_1_fun/ppermute | solution.py:907
  140.4 13.6 %collective-permute-start.13 = (bf16[4,64,768]{2,1,0:T(8,128)(2,1)}, bf16[4,64,768]{2,1,0:T(8,128)(2,1)}, u32[]{:S(2)}, u32[]{:S(2)}) collective-permute-start(bf16[4,64,768]{2,1,0:T(8,128)(2,1)} %get-tuple-element.69), channel_id=1, source_target_pairs={{0,2},{1,3},{2,0},{3,1},{4,6},{5,7},{6,4},{7,5},{8,10},{9,11},{10,... | collective-permute-start | bytes 1179656 | tf_op jit(solution)/shard_map/cond/branch_1_fun/ppermute | solution.py:907
  141.5 12.5 %collective-permute-start.14 = (bf16[4,64,768]{2,1,0:T(8,128)(2,1)}, bf16[4,64,768]{2,1,0:T(8,128)(2,1)}, u32[]{:S(2)}, u32[]{:S(2)}) collective-permute-start(bf16[4,64,768]{2,1,0:T(8,128)(2,1)} %get-tuple-element.69), channel_id=1, source_target_pairs={{0,1},{1,0},{2,3},{3,2},{4,5},{5,4},{6,7},{7,6},{8,9},{9,8},{10,11... | collective-permute-start | bytes 1179656 | tf_op jit(solution)/shard_map/cond/branch_1_fun/ppermute | solution.py:907
  143.1 11.0 %collective-permute-start.17 = (bf16[120,768]{1,0:T(8,128)(2,1)}, bf16[120,768]{1,0:T(8,128)(2,1)}, u32[]{:S(2)}, u32[]{:S(2)}) collective-permute-start(bf16[120,768]{1,0:T(8,128)(2,1)} %copy-done.22), channel_id=1, source_target_pairs={{0,12},{4,8},{8,4},{12,0},{16,28},{20,24},{24,20},{28,16},{1,13},{... | collective-permute-start | bytes 552968 | tf_op jit(solution)/shard_map/cond/branch_1_fun/ppermute | solution.py:907
  154.1 13.5 %collective-permute-start.47 = (bf16[4,64,768]{2,1,0:T(8,128)(2,1)}, bf16[4,64,768]{2,1,0:T(8,128)(2,1)S(1)}, u32[]{:S(2)}, u32[]{:S(2)}) collective-permute-start(bf16[4,64,768]{2,1,0:T(8,128)(2,1)} %get-tuple-element.301.refs_5_), channel_id=1, source_target_pairs={{0,1},{1,0},{2,3},{3,2},{4,5},{5,4},{6,7},{7,6},{8,9},{9,8},{10,11... | collective-permute-start | bytes 1179656 | tf_op jit(solution)/shard_map/ppermute | solution.py:907
  154.1 18.6 %collective-permute-start.50 = (bf16[192,768]{1,0:T(8,128)(2,1)}, bf16[192,768]{1,0:T(8,128)(2,1)S(1)}, u32[]{:S(2)}, u32[]{:S(2)}) collective-permute-start(bf16[192,768]{1,0:T(8,128)(2,1)} %copy-done.20), channel_id=1, source_target_pairs={{0,4},{4,0},{8,12},{12,8},{16,20},{20,16},{24,28},{28,24},{1,5},{5... | collective-permute-start | bytes 884744 | tf_op jit(solution)/shard_map/ppermute | solution.py:907
  154.7 18.0 %collective-permute-start.51 = (bf16[192,768]{1,0:T(8,128)(2,1)}, bf16[192,768]{1,0:T(8,128)(2,1)S(1)}, u32[]{:S(2)}, u32[]{:S(2)}) collective-permute-start(bf16[192,768]{1,0:T(8,128)(2,1)} %copy-done.20), channel_id=1, source_target_pairs={{0,8},{4,12},{8,0},{12,4},{16,24},{20,28},{24,16},{28,20},{1,9},{5... | collective-permute-start | bytes 884744 | tf_op jit(solution)/shard_map/ppermute | solution.py:907
  155.4 17.3 %collective-permute-start.52 = (bf16[192,768]{1,0:T(8,128)(2,1)}, bf16[192,768]{1,0:T(8,128)(2,1)S(1)}, u32[]{:S(2)}, u32[]{:S(2)}) collective-permute-start(bf16[192,768]{1,0:T(8,128)(2,1)} %copy-done.20), channel_id=1, source_target_pairs={{0,12},{4,8},{8,4},{12,0},{16,28},{20,24},{24,20},{28,16},{1,13},{... | collective-permute-start | bytes 884744 | tf_op jit(solution)/shard_map/ppermute | solution.py:907
  166.6 15.2 %collective-permute-start.49 = (f32[8,768]{1,0:T(8,128)S(1)}, f32[8,768]{1,0:T(8,128)S(1)}, u32[]{:S(2)}, u32[]{:S(2)}) collective-permute-start(f32[8,768]{1,0:T(8,128)S(1)} %add_small.1.refs_1_), channel_id=1, source_target_pairs={{0,2},{1,3},{2,0},{3,1},{4,6},{5,7},{6,4},{7,5},{8,10},{9,11},{10,... | collective-permute-start | bytes 73736 | tf_op jit(solution)/shard_map/ppermute | solution.py:907
  (56 other events, 323.1 us)
